TPU v7x, 256 devices: a whole 4x4x8 slice. The times are simulated.
256 devices in a mesh: dp: 32 (over x, z_lo, y), tensor: 8 (over z_hi, core).
Axes of the slice: x: 4, y: 4, z: 8 (z_hi: 4, z_lo: 2; z = z_hi * 2 + z_lo), core: 2. Of those that a mesh axis runs over, the one named last changes fastest.
Arguments:
- tokens: bfloat16 [2560, 2048], P('dp', 'tensor'), may hold values from -6 to 6
- gate_weight: bfloat16 [2048, 8192], P('tensor', 'dp'), may hold values from -0.125 to 0.125
- up_weight: bfloat16 [2048, 8192], P('tensor', 'dp'), may hold values from -0.125 to 0.125
- down_weight: bfloat16 [8192, 2048], P('dp', 'tensor'), may hold values from -0.0625 to 0.0625
- out_grad: bfloat16 [2560, 2048], P('dp', 'tensor'), may hold values from -6 to 6
Outputs:
- mixed: float32 [2560, 2048], P('dp', 'tensor')
- grad_tokens: float32 [2560, 2048], P('dp', 'tensor')
- grad_gate: bfloat16 [2048, 8192], P('tensor', 'dp')
- grad_up: bfloat16 [2048, 8192], P('tensor', 'dp')
- grad_down: bfloat16 [8192, 2048], P('dp', 'tensor')
All inputs are finite; a program needn't handle non-finite values.
Results may differ from a plain program's by a relative error of at most 0.0073.
Values may be sent and summed in bfloat16 or wider, within the bound.
A program may use at most 64 MiB of HBM per device.

v0:
```python
import math

import jax
import jax.numpy as jnp
from jax import lax
from jax.sharding import PartitionSpec as P

D = 2048


def swapped(block, axis, apart):
    count = lax.axis_size(axis)
    route = []
    for low in range(count):
        high = low | 1 << apart
        if high != low and high < count:
            route += [(low, high), (high, low)]
    return lax.ppermute(block, axis, route)


def sylvester_table(order):
    rows = jnp.arange(order, dtype=jnp.int32)[:, None]
    cols = jnp.arange(order, dtype=jnp.int32)[None, :]
    signs = jnp.ones((order, order), jnp.float32)
    for level in range(order.bit_length() - 1):
        bit_on = jnp.bitwise_and(
            jnp.bitwise_and(jnp.right_shift(rows, level), jnp.right_shift(cols, level)), 1
        )
        signs = signs * (1.0 - 2.0 * bit_on.astype(jnp.float32))
    return signs


def rotate_rows(values):
    count = values.shape[0]
    width = values.shape[1]
    lanes = min(width, 128)
    blocks = width // lanes
    shaped = values.reshape(count, blocks, lanes)
    shaped = jnp.einsum(
        "rab,ac->rcb", shaped, sylvester_table(blocks), precision=lax.Precision.HIGHEST
    )
    shaped = jnp.einsum(
        "rcb,bd->rcd", shaped, sylvester_table(lanes), precision=lax.Precision.HIGHEST
    )
    local_rot = shaped.reshape(count, width) * (1.0 / math.sqrt(D))
    groups = lax.axis_size("tensor")
    my_index = lax.axis_index("tensor")
    current = local_rot
    for level in range(groups.bit_length() - 1):
        partner = swapped(current, "tensor", level)
        upper = jnp.bitwise_and(jnp.right_shift(my_index, level), 1) == 1
        current = jnp.where(upper, partner - current, current + partner)
    return current


def contract_last(left, right):
    return lax.dot_general(
        left, right, (((1,), (1,)), ((), ())), preferred_element_type=jnp.float32
    )


def contract_first(left, right):
    return lax.dot_general(
        left, right, (((0,), (0,)), ((), ())), preferred_element_type=jnp.float32
    )


def swiglu_grads(grad_hidden, gate, up):
    sigma = jax.nn.sigmoid(gate)
    grad_gate_act = (grad_hidden * up * sigma * (1.0 + gate * (1.0 - sigma))).astype(jnp.bfloat16)
    grad_up_act = (grad_hidden * gate * sigma).astype(jnp.bfloat16)
    return (grad_gate_act, grad_up_act)


def shards(tokens, gate_weight, up_weight, down_weight, out_grad):
    rotated = rotate_rows(tokens.astype(jnp.float32)).astype(jnp.bfloat16)
    grad_rot = rotate_rows(out_grad.astype(jnp.float32)).astype(jnp.bfloat16)
    inputs_all = lax.all_gather(rotated, "dp", axis=0, tiled=True)
    grads_all = lax.all_gather(grad_rot, "dp", axis=0, tiled=True)
    gate_part = jnp.dot(inputs_all, gate_weight, preferred_element_type=jnp.float32)
    up_part = jnp.dot(inputs_all, up_weight, preferred_element_type=jnp.float32)
    grad_part = contract_last(grads_all, down_weight)
    gate, up, grad_hidden = lax.psum((gate_part, up_part, grad_part), "tensor")
    hidden = (jax.nn.silu(gate) * up).astype(jnp.bfloat16)
    grad_gate_act, grad_up_act = swiglu_grads(grad_hidden, gate, up)
    output_sums = lax.psum_scatter(
        jnp.dot(hidden, down_weight, preferred_element_type=jnp.float32),
        "dp",
        scatter_dimension=0,
        tiled=True,
    )
    mixed = rotate_rows(output_sums)
    input_sums = lax.psum_scatter(
        contract_last(grad_gate_act, gate_weight) + contract_last(grad_up_act, up_weight),
        "dp",
        scatter_dimension=0,
        tiled=True,
    )
    grad_tokens = rotate_rows(input_sums)
    factor = 1.0 / math.sqrt(inputs_all.shape[0])
    grad_gate = (contract_first(inputs_all, grad_gate_act) * factor).astype(jnp.bfloat16)
    grad_up = (contract_first(inputs_all, grad_up_act) * factor).astype(jnp.bfloat16)
    grad_down = (contract_first(hidden, grads_all) * factor).astype(jnp.bfloat16)
    return (mixed, grad_tokens, grad_gate, grad_up, grad_down)


def solution(mesh):
    return jax.shard_map(
        shards,
        mesh=mesh,
        in_specs=(
            P("dp", "tensor"),
            P("tensor", "dp"),
            P("tensor", "dp"),
            P("dp", "tensor"),
            P("dp", "tensor"),
        ),
        out_specs=(
            P("dp", "tensor"),
            P("dp", "tensor"),
            P("tensor", "dp"),
            P("tensor", "dp"),
            P("dp", "tensor"),
        ),
        check_vma=False,
    )
```

profile of v0, /device:TPU:1, one launch (start us, length us, event | category | flops | bytes accessed | tf_op | source)
XLA Modules:
  0.0 897.4 jit_solution(4612303353981806699)
XLA Ops:
  8.9 3.3 collective-permute-start
  14.5 5.5 collective-permute-done.1
  20.1 5.1 collective-permute-start.2
  25.1 2.2 collective-permute-done.2
  28.9 2.8 collective-permute-start.6
  32.8 6.8 collective-permute-done.7
  39.7 3.9 collective-permute-start.8
  43.5 4.9 collective-permute-done.8
  49.2 114.7 %all-gather.3.cloned.1.call-done = bf16[2560,256]{1,0:T(8,128)(2,1)} async-done(((bf16[80,256]{1,0:T(8,128)(2,1)}), bf16[2560,256]{1,0:T(8,128)(2,1)}) %all-gather.3.cloned.1.call-update) | async-done | bytes 1310736 | tf_op jit(solution)/shard_map/all_gather | solution.py:78
  163.9 3.5 fusion.48
  169.5 150.2 %all-gather.5.cloned.1.call-done = bf16[2560,256]{1,0:T(8,128)(2,1)} async-done(((bf16[80,256]{1,0:T(8,128)(2,1)}), bf16[2560,256]{1,0:T(8,128)(2,1)}) %all-gather.5.cloned.1.call-update) | async-done | bytes 1310736 | tf_op jit(solution)/shard_map/all_gather | solution.py:79
  319.7 3.3 fusion.50
  323.1 202.5 %all-reduce.3.cloned.1.call-done = (f32[2560,256]{1,0:T(8,128)}, f32[2560,256]{1,0:T(8,128)}, f32[2560,256]{1,0:T(8,128)}) async-done(((f32[2560,256]{1,0:T(8,128)}, f32[2560,256]{1,0:T(8,128)}, f32[2560,256]{1,0:T(8,128)}), (f32[2560,256]{1,0:T(8,128)}, f32[2560,256]{1,0:T(8,128)}, f32[2560,256]{1,0:T(8,128)})) %all-reduce.3.cloned.1.call-update) | async-done | bytes 7864336 | tf_op jit(solution)/shard_map/psum | solution.py:83
  525.7 4.9 multiply_convert_fusion
  531.6 2.1 convolution_add_fusion
  533.7 3.3 fusion.49
  537.1 2.9 fusion.2
  542.5 137.1 %reduce-scatter.5.cloned.1.call-done = f32[80,256]{1,0:T(8,128)} async-done(((f32[2560,256]{1,0:T(8,128)}), f32[80,256]{1,0:T(8,128)}) %reduce-scatter.5.cloned.1.call-update) | async-done | bytes 81936 | tf_op jit(solution)/shard_map/reduce_scatter | solution.py:93
  681.6 24.2 %collective-permute-start.9 = (f32[80,256]{1,0:T(8,128)S(1)}, f32[80,256]{1,0:T(8,128)S(1)}, u32[]{:S(2)}, u32[]{:S(2)}) collective-permute-start(f32[80,256]{1,0:T(8,128)S(1)} %bitcast.77), channel_id=1, source_target_pairs={{0,1},{1,0},{2,3},{3,2},{4,5},{5,4},{6,7},{7,6},{8,9},{9,8},{10,11... | collective-permute-start | bytes 245768 | tf_op jit(solution)/shard_map/ppermute | solution.py:18
  705.8 139.2 %reduce-scatter.3.cloned.1.call-done = f32[80,256]{1,0:T(8,128)} async-done(((f32[2560,256]{1,0:T(8,128)}), f32[80,256]{1,0:T(8,128)}) %reduce-scatter.3.cloned.1.call-update) | async-done | bytes 81936 | tf_op jit(solution)/shard_map/reduce_scatter | solution.py:86
  846.9 25.6 %collective-permute-start.3 = (f32[80,256]{1,0:T(8,128)S(1)}, f32[80,256]{1,0:T(8,128)S(1)}, u32[]{:S(2)}, u32[]{:S(2)}) collective-permute-start(f32[80,256]{1,0:T(8,128)S(1)} %bitcast.79), channel_id=1, source_target_pairs={{0,1},{1,0},{2,3},{3,2},{4,5},{5,4},{6,7},{7,6},{8,9},{9,8},{10,11... | collective-permute-start | bytes 245768 | tf_op jit(solution)/shard_map/ppermute | solution.py:18
  875.0 3.4 collective-permute-done.10
  878.4 2.9 collective-permute-start.11
  882.9 4.8 collective-permute-start.5
  (72 shorter events, 24.1 us)
Async XLA Ops:
  7.2 160.2 %copy-start = (bf16[256,256]{1,0:T(8,128)(2,1)S(1)}, bf16[256,256]{1,0:T(8,128)(2,1)}, u32[]{:S(2)}) copy-start(bf16[256,256]{1,0:T(8,128)(2,1)} %param.6) | copy-start | bytes 393220
  7.2 20.9 %copy-start.6 = (bf16[80,256]{1,0:T(8,128)(2,1)S(1)}, bf16[80,256]{1,0:T(8,128)(2,1)}, u32[]{:S(2)}) copy-start(bf16[80,256]{1,0:T(8,128)(2,1)} %param.9) | copy-start | bytes 122884
  7.2 156.7 %all-gather.3.cloned.1.call-start = ((), (), s32[]{:S(2)}) async-start(), calls=%async_computation.2 | async-start | bytes 1351680 | tf_op jit(solution)/shard_map/all_gather | solution.py:78
  8.9 155.0 %copy-start.4 = (bf16[256,256]{1,0:T(8,128)(2,1)S(1)}, bf16[256,256]{1,0:T(8,128)(2,1)}, u32[]{:S(2)}) copy-start(bf16[256,256]{1,0:T(8,128)(2,1)} %param.7) | copy-start | bytes 393220
  8.9 4.3 collective-permute-start
  13.2 6.9 collective-permute-start.1
  20.1 7.3 collective-permute-start.2
  28.0 291.7 %all-gather.5.cloned.1.call-start = ((), (), s32[]{:S(2)}) async-start(), calls=%async_computation.4 | async-start | bytes 1351680 | tf_op jit(solution)/shard_map/all_gather | solution.py:79
  28.9 3.8 collective-permute-start.6
  32.7 6.9 collective-permute-start.7
  39.7 8.8 collective-permute-start.8
  49.1 476.5 %all-reduce.3.cloned.1.call-start = ((), (), s32[]{:S(2)}) async-start(), calls=%async_computation.6 | async-start | bytes 15728640 | tf_op jit(solution)/shard_map/psum | solution.py:83
  163.9 3.5 copy-start.1
  167.4 152.3 %copy-start.5 = (bf16[256,256]{1,0:T(8,128)(2,1)S(1)}, bf16[256,256]{1,0:T(8,128)(2,1)}, u32[]{:S(2)}) copy-start(bf16[256,256]{1,0:T(8,128)(2,1)} %param.8) | copy-start | bytes 393220
  323.1 356.6 %reduce-scatter.5.cloned.1.call-start = ((), (), s32[]{:S(2)}) async-start(), calls=%async_computation.5 | async-start | bytes 2703360 | tf_op jit(solution)/shard_map/reduce_scatter | solution.py:93
  530.5 1.1 copy-start.2
  533.7 311.2 %reduce-scatter.3.cloned.1.call-start = ((), (), s32[]{:S(2)}) async-start(), calls=%async_computation.3 | async-start | bytes 2703360 | tf_op jit(solution)/shard_map/reduce_scatter | solution.py:86
  540.0 1.3 copy-start.3
  681.6 190.8 %collective-permute-start.9 = (f32[80,256]{1,0:T(8,128)S(1)}, f32[80,256]{1,0:T(8,128)S(1)}, u32[]{:S(2)}, u32[]{:S(2)}) collective-permute-start(f32[80,256]{1,0:T(8,128)S(1)} %bitcast.77), channel_id=1, source_target_pairs={{0,1},{1,0},{2,3},{3,2},{4,5},{5,4},{6,7},{7,6},{8,9},{9,8},{10,11... | collective-permute-start | bytes 245768 | tf_op jit(solution)/shard_map/ppermute | solution.py:18
  846.9 26.5 %collective-permute-start.3 = (f32[80,256]{1,0:T(8,128)S(1)}, f32[80,256]{1,0:T(8,128)S(1)}, u32[]{:S(2)}, u32[]{:S(2)}) collective-permute-start(f32[80,256]{1,0:T(8,128)S(1)} %bitcast.79), channel_id=1, source_target_pairs={{0,1},{1,0},{2,3},{3,2},{4,5},{5,4},{6,7},{7,6},{8,9},{9,8},{10,11... | collective-permute-start | bytes 245768 | tf_op jit(solution)/shard_map/ppermute | solution.py:18
  872.4 6.0 collective-permute-start.10
  873.4 9.5 %collective-permute-start.4 = (f32[80,256]{1,0:T(8,128)S(1)}, f32[80,256]{1,0:T(8,128)S(1)}, u32[]{:S(2)}, u32[]{:S(2)}) collective-permute-start(f32[80,256]{1,0:T(8,128)S(1)} %add_select_fusion.7), channel_id=1, source_target_pairs={{0,2},{2,0},{1,3},{3,1},{4,6},{6,4},{5,7},{7,5},{8,10},{10,8},{9,1... | collective-permute-start | bytes 245768 | tf_op jit(solution)/shard_map/ppermute | solution.py:18
  878.4 9.3 %collective-permute-start.11 = (f32[80,256]{1,0:T(8,128)S(1)}, f32[80,256]{1,0:T(8,128)S(1)}, u32[]{:S(2)}, u32[]{:S(2)}) collective-permute-start(f32[80,256]{1,0:T(8,128)S(1)} %add_select_fusion.1), channel_id=1, source_target_pairs={{0,4},{4,0},{1,5},{5,1},{2,6},{6,2},{3,7},{7,3},{8,12},{12,8},{9,1... | collective-permute-start | bytes 245768 | tf_op jit(solution)/shard_map/ppermute | solution.py:18
  882.9 7.3 collective-permute-start.5
Sparse Core Ops, SparseCore 0:
  28.2 135.6 all-gather.2
  166.3 153.4 all-gather.4
  323.2 202.3 all-reduce.2
  533.8 145.8 reduce-scatter.4
  682.0 162.8 reduce-scatter.2
where the time goes:
time: 898 us; the launch traced here: 897 us
  waiting for transfers between devices  772 us (86%)
  starting transfers between devices  76.7 us (9%)
  matrix products  23.8 us (3%)
  between operations  14 us (2%)
    psum x1, waiting for transfers between devices, shards(): gate, up, grad_hidden = lax.psum((gate_part, up_part, grad_part), 'tensor')  203 us
    all_gather x1, waiting for transfers between devices, shards(): grads_all = lax.all_gather(grad_rot, 'dp', axis=0, tiled=True)  150 us
    reduce_scatter x1, waiting for transfers between devices, shards(): lax.psum_scatter(jnp.dot(hidden, down_weight, preferred_element_type=jnp....  139 us
    reduce_scatter x1, waiting for transfers between devices, shards(): lax.psum_scatter(contract_last(grad_gate_act, gate_weight) + contract_las...  137 us
    all_gather x1, waiting for transfers between devices, shards(): inputs_all = lax.all_gather(rotated, 'dp', axis=0, tiled=True)  115 us
    ppermute x12, starting transfers between devices, swapped(): return lax.ppermute(block, axis, route)  76.5 us
    ppermute x12, waiting for transfers between devices, swapped(): return lax.ppermute(block, axis, route)  28.2 us
  transfers between devices with their start and end apart: 17, of which 14 were waited for; matrix products, arithmetic and copies ran while one was open for 2% of the time, Pallas kernels for 0%

commit v1 on v0

v1 whole, which is shorter than its diff:
```python
import math

import jax
import jax.numpy as jnp
from jax import lax
from jax.experimental import pallas as pl
from jax.experimental.pallas import tpu as pltpu
from jax.sharding import PartitionSpec as P

D = 2048
TOKENS = 2560
ROWS = 80
LANES = 256
UNITS = 64
MESH = pl.DeviceIdType.MESH
F32 = jnp.float32
BF16 = jnp.bfloat16


def dot_nn(a, b):
    return lax.dot_general(a, b, (((1,), (0,)), ((), ())), preferred_element_type=F32)


def dot_nt(a, b):
    return lax.dot_general(a, b, (((1,), (1,)), ((), ())), preferred_element_type=F32)


def butterflies(parts):
    parts = list(parts)
    for bit in range(3):
        step = 1 << bit
        for low in range(8):
            if not low & step:
                a, b = parts[low], parts[low | step]
                parts[low], parts[low | step] = a + b, a - b
    return parts


def kernel(tok, og, gw, uw, dw, mixed, gtok, gg, gu, gd,
           AB, PK, WB, H, FS, ROT, HID, GACT, MP, R1, R2, ZS, ZR,
           WO, CS, CR, XS, X1, X2, ZW, ZWR, GTT,
           zs, zr, ws, wr, ys, yr, y2s, y2r, xs, xr, x2s, x2r, cs, cr, os_, or_, os2, or2,
           es, er, gs, gr, vs, vr):
    dp = lax.axis_index("dp")
    te = lax.axis_index("tensor")
    x, zl, y = dp // 8, (dp // 4) % 2, dp % 4
    zh, c = te // 2, te % 2
    z = 2 * zh + zl
    k_own = te
    other = 1 - c
    home = c == zl
    xp, xm, xf = (x + 1) % 4, (x + 3) % 4, (x + 2) % 4
    yp, ym, yf = (y + 1) % 4, (y + 3) % 4, (y + 2) % 4

    def did(x_, y_, z_, c_):
        return ((x_ * 2 + z_ % 2) * 4 + y_, (z_ // 2) * 2 + c_)

    def rc(src, dst, send, recv, dev):
        return pltpu.make_async_remote_copy(
            src_ref=src, dst_ref=dst, send_sem=send, recv_sem=recv,
            device_id=dev, device_id_type=MESH)

    here = did(x, y, z, other)
    dev_x = (did(xp, y, z, c), did(xm, y, z, c))
    dev_y = (did(x, yp, z, c), did(x, ym, z, c))
    sent = []

    def start(src, dst, send, recv, dev):
        cp = rc(src, dst, send, recv, dev)
        cp.start()
        sent.append(cp)

    def arrive(dst, recv):
        rc(dst, dst, recv, recv, here).wait_recv()

    barrier = pltpu.get_barrier_semaphore()

    def greet(dev):
        pl.semaphore_signal(barrier, inc=1, device_id=dev, device_id_type=MESH)

    for dz in range(8):
        for cc in range(2):
            if dz or cc:
                greet(did(x, y, (z + dz) % 8, (c + cc) % 2))
    for dev in dev_x + dev_y:
        greet(dev)

    gwt = gw[...].astype(F32).T.astype(BF16)
    uwt = uw[...].astype(F32).T.astype(BF16)
    for q in range(4):
        PK[q, 0:UNITS] = gwt[q * UNITS:(q + 1) * UNITS]
        PK[q, UNITS:2 * UNITS] = uwt[q * UNITS:(q + 1) * UNITS]
        PK[q, 2 * UNITS:3 * UNITS] = dw[q * UNITS:(q + 1) * UNITS, :]
    i = lax.broadcasted_iota(jnp.int32, (LANES, LANES), 0)
    j = lax.broadcasted_iota(jnp.int32, (LANES, LANES), 1)
    b = i & j
    b = b ^ (b >> 4)
    b = b ^ (b >> 2)
    b = (b ^ (b >> 1)) & 1
    H[...] = (1 - 2 * b).astype(F32).astype(BF16)
    WB[x, c, zh] = PK[zh]

    pl.semaphore_wait(barrier, 19)

    def send_tokens(a, ref):
        for dz in (1, 7, 0, 2, 6, 3, 5, 4):
            cp = rc(ref, AB.at[a, y, k_own], zs.at[a, dz], zr.at[a, k_own],
                    did(x, y, (z + dz) % 8, zl))
            if dz:
                cp.start()
                sent.append(cp)
            else:
                @pl.when(home)
                def _():
                    AB[a, y, k_own] = ref[...]

                @pl.when(jnp.logical_not(home))
                def _():
                    cp.start()

    def send_weights():
        for q in (1, 3, 2):
            to = (zh + q) % 4
            start(PK.at[to], WB.at[x, c, zh], ws.at[q], wr.at[q], did(x, y, 2 * to + zl, c))

    send_tokens(0, tok)
    send_weights()
    send_tokens(1, og)

    order = (0, 1, 3, 2)

    def pair(a, yy, pos):
        return AB.at[a, yy, pl.ds(2 * ((zh + order[pos]) % 4), 2)]

    def tokens_z(a):
        for pos in range(4):
            from_zh = (zh + order[pos]) % 4
            k_same, k_other = 2 * from_zh + c, 2 * from_zh + other
            arrive(AB.at[a, y, k_other], zr.at[a, k_other])
            if pos == 0:
                @pl.when(jnp.logical_not(home))
                def _():
                    arrive(AB.at[a, y, k_same], zr.at[a, k_same])
            else:
                arrive(AB.at[a, y, k_same], zr.at[a, k_same])
            for way in range(2):
                start(pair(a, y, pos), pair(a, y, pos), ys.at[a, pos, way], yr.at[a, pos, way], dev_y[way])

    def weights_z():
        for q in (0, 1, 3, 2):
            frm = (zh + 4 - q) % 4
            if q:
                arrive(WB.at[x, c, frm], wr.at[q])
            for way in range(2):
                start(WB.at[x, c, frm], WB.at[x, c, frm], xs.at[q, way], xr.at[q, way], dev_x[way])
        start(WB.at[x, c], WB.at[x, c], cs.at[0], cr.at[0], here)

    def tokens_y(a):
        for pos in range(4):
            for way in range(2):
                frm = (ym, yp)[way]
                arrive(pair(a, frm, pos), yr.at[a, pos, way])
                if (pos < 2) == (way == 0):
                    start(pair(a, frm, pos), pair(a, frm, pos), y2s.at[a, pos], y2r.at[a, pos], dev_y[way])

    def weights_x():
        for way in range(2):
            frm = (xm, xp)[way]
            for q in (0, 1, 3, 2):
                arrive(WB.at[frm, c, (zh + 4 - q) % 4], xr.at[q, way])
            half = WB.at[frm, c, pl.ds(2 * way, 2)]
            start(half, half, x2s.at[way], x2r.at[way], dev_x[way])
            start(WB.at[frm, c], WB.at[frm, c], cs.at[1 + way], cr.at[1 + way], here)

    def weights_far():
        for way in range(2):
            arrive(WB.at[xf, c, pl.ds(2 * way, 2)], x2r.at[way])
        start(WB.at[xf, c], WB.at[xf, c], cs.at[3], cr.at[3], here)
        for n, frm in enumerate((x, xm, xp, xf)):
            arrive(WB.at[frm, other], cr.at[n])

    scale = 1.0 / math.sqrt(D)

    def spread(a, yy):
        def step(r, _):
            rows = pl.ds(pl.multiple_of(r * 16, 16), 16)
            parts = butterflies([FS[k, rows] for k in range(8)])
            for k in range(8):
                ROT[a, k, yy, rows] = (parts[k] * scale).astype(BF16)
            return 0
        lax.fori_loop(0, ROWS // 16, step, 0)

    def rotate_in(a, yy):
        FS[...] = dot_nn(AB[a, yy].reshape(8 * ROWS, LANES), H[...]).reshape(8, ROWS, LANES)
        spread(a, yy)

    def tokens_far(a):
        for pos in range(4):
            arrive(pair(a, yf, pos), y2r.at[a, pos])
        rotate_in(a, yf)

    tokens_z(0)
    weights_z()
    tokens_z(1)
    rotate_in(0, y)
    tokens_y(0)
    rotate_in(0, ym)
    rotate_in(0, yp)
    weights_x()
    tokens_y(1)
    rotate_in(1, y)
    rotate_in(1, ym)
    rotate_in(1, yp)
    tokens_far(0)
    weights_far()

    def rot(a, k):
        return ROT[a, k].reshape(4 * ROWS, LANES)

    def weight(w, k):
        return jnp.concatenate(
            [WB[q, k % 2, k // 2, w * UNITS:(w + 1) * UNITS] for q in range(4)], axis=0)

    rot_tok = jnp.concatenate([rot(0, k) for k in range(8)], axis=1)

    def all_weight(w):
        return jnp.concatenate([weight(w, k) for k in range(8)], axis=1)

    gate = dot_nt(rot_tok, all_weight(0))
    up = dot_nt(rot_tok, all_weight(1))
    sigma = 1.0 / (1.0 + jnp.exp(-gate))
    hidden = (gate * sigma * up).astype(BF16)
    HID[...] = hidden
    GACT[0] = up * sigma * (1.0 + gate * (1.0 - sigma))
    GACT[1] = gate * sigma

    def halves(a):
        lo, hi = pl.ds(0, 4), pl.ds(4, 4)
        start(MP.at[a, yf, lo], R1.at[a, 0], os_.at[a, 0], or_.at[a, 0], dev_y[0])
        start(MP.at[a, yf, hi], R1.at[a, 1], os_.at[a, 1], or_.at[a, 1], dev_y[1])
        start(MP.at[a, yp, hi], R2.at[a, 0, hi], os_.at[a, 2], or_.at[a, 2], dev_y[0])
        start(MP.at[a, ym, lo], R2.at[a, 1, lo], os_.at[a, 3], or_.at[a, 3], dev_y[1])

    def pass_on(a):
        lo, hi = pl.ds(0, 4), pl.ds(4, 4)
        arrive(R1.at[a, 0], or_.at[a, 0])
        MP[a, yp, 0:4] = (MP[a, yp, 0:4].astype(F32) + R1[a, 0].astype(F32)).astype(BF16)
        start(MP.at[a, yp, lo], R2.at[a, 0, lo], os2.at[a, 0], or2.at[a, 0], dev_y[0])
        arrive(R1.at[a, 1], or_.at[a, 1])
        MP[a, ym, 4:8] = (MP[a, ym, 4:8].astype(F32) + R1[a, 1].astype(F32)).astype(BF16)
        start(MP.at[a, ym, hi], R2.at[a, 1, hi], os2.at[a, 1], or2.at[a, 1], dev_y[1])

    def rotate_out(a):
        lo, hi = pl.ds(0, 4), pl.ds(4, 4)
        arrive(R2.at[a, 0, hi], or_.at[a, 2])
        arrive(R2.at[a, 1, lo], or_.at[a, 3])
        arrive(R2.at[a, 0, lo], or2.at[a, 0])
        arrive(R2.at[a, 1, hi], or2.at[a, 1])
        total = MP[a, y].astype(F32) + R2[a, 0].astype(F32) + R2[a, 1].astype(F32)
        total = total.reshape(8 * ROWS, LANES)
        high = total.astype(BF16)
        low = (total - high.astype(F32)).astype(BF16)
        FS[...] = (dot_nn(high, H[...]) + dot_nn(low, H[...])).reshape(8, ROWS, LANES)

        def step(r, _):
            rows = pl.ds(pl.multiple_of(r * 16, 16), 16)
            parts = butterflies([FS[k, rows] for k in range(8)])
            for k in range(8):
                ZS[a, k, rows] = (parts[k] * scale).astype(BF16)
            return 0
        lax.fori_loop(0, ROWS // 16, step, 0)
        for q in (0, 1, 3, 2):
            to = (zh + q) % 4
            for cc in (0, 1):
                to_c = (c + cc) % 2
                src = ZS.at[a, 2 * to + to_c]
                cp = rc(src, ZR.at[a, z], es.at[a, 2 * q + cc], er.at[a, z], did(x, y, 2 * to + c, to_c))
                if q or cc:
                    cp.start()
                    sent.append(cp)
                else:
                    @pl.when(home)
                    def _():
                        ZR[a, z] = ZS[a, 2 * zh + c]

                    @pl.when(jnp.logical_not(home))
                    def _():
                        cp.start()

    def finish_tokens(a, out):
        for dz in range(8):
            frm = (z + dz) % 8
            if dz:
                arrive(ZR.at[a, frm], er.at[a, frm])
            else:
                @pl.when(jnp.logical_not(home))
                def _():
                    arrive(ZR.at[a, frm], er.at[a, frm])
        total = ZR[a, 0].astype(F32)
        for s in range(1, 8):
            total = total + ZR[a, s].astype(F32)
        out[...] = total

    for k in range(8):
        MP[0, :, k] = dot_nn(hidden, weight(2, k)).astype(BF16).reshape(4, ROWS, LANES)
    halves(0)
    tokens_far(1)
    pass_on(0)

    rot_grad = jnp.concatenate([rot(1, k) for k in range(8)], axis=1)
    grad_hidden = dot_nt(rot_grad, all_weight(2))
    gga = grad_hidden * GACT[0]
    gua = grad_hidden * GACT[1]
    gga_b = gga.astype(BF16)
    gua_b = gua.astype(BF16)
    GTT[0] = gga.T.astype(BF16)
    GTT[1] = gua.T.astype(BF16)
    GTT[2] = HID[...].astype(F32).T.astype(BF16)
    for k in range(8):
        MP[1, :, k] = (dot_nn(gga_b, weight(0, k)) + dot_nn(gua_b, weight(1, k))).astype(BF16).reshape(4, ROWS, LANES)
    halves(1)

    def weight_grads(parity, store):
        def step(q, _):
            k = 2 * q + parity
            for w in range(3):
                g = dot_nn(GTT[w], ROT[w // 2, k].reshape(4 * ROWS, LANES))
                for p in range(4):
                    store(p, q, w, g[p * UNITS:(p + 1) * UNITS])
            return 0
        lax.fori_loop(0, 4, step, 0)

    def store_other(p, q, w, g):
        CS[p, q, w * UNITS:(w + 1) * UNITS] = g.astype(BF16)

    def store_own(p, q, w, g):
        WO[p, q, w * UNITS:(w + 1) * UNITS] = g

    weight_grads(other, store_other)
    for n, p in enumerate((xf, xp, xm, x)):
        start(CS.at[p], CR.at[p], cs.at[4 + n], cr.at[4 + n], here)
    pass_on(1)
    weight_grads(c, store_own)

    arrive(CR.at[xf], cr.at[4])
    XS[xf] = (WO[xf] + CR[xf].astype(F32)).astype(BF16)
    lo, hi = pl.ds(0, 2), pl.ds(2, 2)
    start(XS.at[xf, lo], X1.at[0], gs.at[0], gr.at[0], dev_x[0])
    start(XS.at[xf, hi], X1.at[1], gs.at[1], gr.at[1], dev_x[1])
    arrive(CR.at[xp], cr.at[5])
    XS[xp, 2:4] = (WO[xp, 2:4] + CR[xp, 2:4].astype(F32)).astype(BF16)
    start(XS.at[xp, hi], X2.at[0, hi], gs.at[2], gr.at[2], dev_x[0])
    arrive(CR.at[xm], cr.at[6])
    XS[xm, 0:2] = (WO[xm, 0:2] + CR[xm, 0:2].astype(F32)).astype(BF16)
    start(XS.at[xm, lo], X2.at[1, lo], gs.at[3], gr.at[3], dev_x[1])

    rotate_out(0)

    arrive(X1.at[0], gr.at[0])
    XS[xp, 0:2] = (WO[xp, 0:2] + CR[xp, 0:2].astype(F32) + X1[0].astype(F32)).astype(BF16)
    start(XS.at[xp, lo], X2.at[0, lo], gs.at[4], gr.at[4], dev_x[0])
    arrive(X1.at[1], gr.at[1])
    XS[xm, 2:4] = (WO[xm, 2:4] + CR[xm, 2:4].astype(F32) + X1[1].astype(F32)).astype(BF16)
    start(XS.at[xm, hi], X2.at[1, hi], gs.at[5], gr.at[5], dev_x[1])
    arrive(CR.at[x], cr.at[7])

    rotate_out(1)
    finish_tokens(0, mixed)

    arrive(X2.at[0, hi], gr.at[2])
    arrive(X2.at[1, lo], gr.at[3])
    arrive(X2.at[0, lo], gr.at[4])
    arrive(X2.at[1, hi], gr.at[5])
    factor = 1.0 / math.sqrt(TOKENS)
    for q in range(4):
        total = WO[x, q] + CR[x, q].astype(F32) + X2[0, q].astype(F32) + X2[1, q].astype(F32)
        ZW[q] = (total * factor).astype(BF16)
    for q in (1, 3, 2):
        to = (zh + q) % 4
        start(ZW.at[to], ZWR.at[zh], vs.at[q], vr.at[q], did(x, y, 2 * to + zl, c))
    ZWR[zh] = ZW[zh]

    finish_tokens(1, gtok)

    for q in (1, 3, 2):
        arrive(ZWR.at[(zh + 4 - q) % 4], vr.at[q])
    for w, out in ((0, gg), (1, gu)):
        rows = jnp.concatenate([ZWR[q, w * UNITS:(w + 1) * UNITS] for q in range(4)], axis=0)
        out[...] = rows.astype(F32).T.astype(BF16)
    for q in range(4):
        gd[q * UNITS:(q + 1) * UNITS, :] = ZWR[q, 2 * UNITS:3 * UNITS]

    for cp in sent:
        cp.wait_send()

    @pl.when(jnp.logical_not(home))
    def _():
        for a, ref in ((0, tok), (1, og)):
            rc(ref, AB.at[a, y, k_own], zs.at[a, 0], zr.at[a, k_own], here).wait_send()
            rc(ZS.at[a, 0], ZR.at[a, z], es.at[a, 0], er.at[a, z], here).wait_send()


def shards(tokens, gate_weight, up_weight, down_weight, out_grad):
    dma = pltpu.SemaphoreType.DMA
    vm = pltpu.VMEM
    block = jax.ShapeDtypeStruct
    rows, cols = tokens.shape
    return pl.pallas_call(
        kernel,
        out_shape=(
            block((ROWS, LANES), F32), block((ROWS, LANES), F32),
            block((256, 256), BF16), block((256, 256), BF16), block((256, 256), BF16)),
        in_specs=[pl.BlockSpec(memory_space=vm)] * 5,
        out_specs=[pl.BlockSpec(memory_space=vm)] * 5,
        scratch_shapes=[
            vm((2, 4, 8, ROWS, LANES), BF16),
            vm((4, 192, LANES), BF16),
            vm((4, 2, 4, 192, LANES), BF16),
            vm((LANES, LANES), BF16),
            vm((8, ROWS, LANES), F32),
            vm((2, 8, 4, ROWS, LANES), BF16),
            vm((4 * ROWS, 256), BF16),
            vm((2, 4 * ROWS, 256), F32),
            vm((2, 4, 8, ROWS, LANES), BF16),
            vm((2, 2, 4, ROWS, LANES), BF16),
            vm((2, 2, 8, ROWS, LANES), BF16),
            vm((2, 8, ROWS, LANES), BF16),
            vm((2, 8, ROWS, LANES), BF16),
            vm((4, 4, 192, LANES), F32),
            vm((4, 4, 192, LANES), BF16),
            vm((4, 4, 192, LANES), BF16),
            vm((4, 4, 192, LANES), BF16),
            vm((2, 2, 192, LANES), BF16),
            vm((2, 4, 192, LANES), BF16),
            vm((4, 192, LANES), BF16),
            vm((4, 192, LANES), BF16),
            vm((3, 256, 4 * ROWS), BF16),
            dma((2, 8)), dma((2, 8)), dma((4,)), dma((4,)),
            dma((2, 4, 2)), dma((2, 4, 2)), dma((2, 4)), dma((2, 4)),
            dma((4, 2)), dma((4, 2)), dma((2,)), dma((2,)),
            dma((8,)), dma((8,)), dma((2, 4)), dma((2, 4)), dma((2, 2)), dma((2, 2)),
            dma((2, 8)), dma((2, 8)), dma((6,)), dma((6,)), dma((4,)), dma((4,)),
        ],
        compiler_params=pltpu.CompilerParams(
            collective_id=0, has_side_effects=True, vmem_limit_bytes=48 << 20),
        name="layer",
    )(tokens, out_grad, gate_weight, up_weight, down_weight)


def solution(mesh):
    return jax.shard_map(
        shards,
        mesh=mesh,
        in_specs=(P("dp", "tensor"), P("tensor", "dp"), P("tensor", "dp"), P("dp", "tensor"), P("dp", "tensor")),
        out_specs=(P("dp", "tensor"), P("dp", "tensor"), P("tensor", "dp"), P("tensor", "dp"), P("dp", "tensor")),
        check_vma=False,
    )
```

time: 898 us -> 102 us (0.11)
  waiting for transfers between devices: 772 us -> 0 us
  Pallas kernels: 0 us -> 91.9 us
  starting transfers between devices: 76.7 us -> 0 us
  matrix products: 23.8 us -> 0 us
  between operations: 14 us -> 0.66 us
    reduce_scatter x2 -> x0, waiting for transfers between devices: 276 us -> none  [the longest x1 139 us: shards(): lax.psum_scatter(jnp.dot(hidden, down_weight, preferred_element_type=jnp....]
    all_gather x2 -> x0, waiting for transfers between devices: 265 us -> none  [the longest x1 150 us: shards(): grads_all = lax.all_gather(grad_rot, 'dp', axis=0, tiled=True)]
    psum x1 -> x0, waiting for transfers between devices: 203 us -> none  [shards(): gate, up, grad_hidden = lax.psum((gate_part, up_part, grad_part), 'tensor')]
    pallas_call x0 -> x1, Pallas kernels: none -> 91.9 us  [shards(): pl.pallas_call(kernel, out_shape=(block((ROWS, LANES), F32), block((ROWS,...]
    ppermute x12 -> x0, starting transfers between devices: 76.5 us -> none  [swapped(): return lax.ppermute(block, axis, route)]
    ppermute x12 -> x0, waiting for transfers between devices: 28.2 us -> none  [swapped(): return lax.ppermute(block, axis, route)]
    dot_general x17 -> x0, matrix products: 23.8 us -> none  [the longest x3 5.98 us: contract_last(): lax.dot_general(left, right, (((1,), (1,)), ((), ())), preferred_element_...]
  transfers between devices with their start and end apart: 17 -> 0, of which waited for: 14 -> 0; matrix products, arithmetic and copies ran while one was open for 2% -> 0% of each run, Pallas kernels for 0% -> 0%
where the time goes in v1:
time: 102 us; the launch traced here: 100 us
  Pallas kernels  91.9 us (90%)
  local copies, waits for them, and re-layouts  7.5 us (7%)
    pallas_call x1, Pallas kernels, shards(): pl.pallas_call(kernel, out_shape=(block((ROWS, LANES), F32), block((ROWS,...  91.9 us
    unnamed x15, local copies, waits for them, and re-layouts  7.5 us

profile of v1, /device:TPU:1, one launch (start us, length us, event | category | flops | bytes accessed | tf_op | source)
XLA Modules:
  0.0 100.0 jit_solution(16739642007132820217)
XLA Ops:
  0.6 0.0 copy-start
  0.6 0.9 copy-done
  1.5 0.0 copy-start.1
  1.5 0.9 copy-done.1
  2.4 0.0 copy-start.2
  2.4 0.9 copy-done.2
  3.3 0.0 copy-start.3
  3.3 0.8 copy-done.3
  4.1 0.0 copy-start.4
  4.1 0.8 copy-done.4
  4.9 91.9 %layer.1 = (f32[80,256]{1,0:T(8,128)S(1)}, f32[80,256]{1,0:T(8,128)S(1)}, bf16[256,256]{1,0:T(8,128)(2,1)S(1)}, bf16[256,256]{1,0:T(8,128)(2,1)S(1)}, bf16[256,256]{1,0:T(8,128)(2,1)S(1)}) custom-call(bf16[80,256]{1,0:T(8,128)(2,1)S(1)} %copy-done.3, bf16[80,256]{1,0:T(8,128)(2,1)S(1)} %copy-done.4, bf16[256,256]{1,0:T(8,128)(2,1)S(1)} %copy-done, ...), custom_call_target="tpu_custom_call" | custom-call | tf_op jit(solution)/shard_map/layer/pallas_call | solution.py:408
  96.8 0.6 copy.15
  97.4 0.6 copy.16
  98.1 0.7 copy.17
  98.7 0.7 copy.18
  99.4 0.7 copy.19
Async XLA Ops:
  0.6 0.9 copy-start
  1.5 0.9 copy-start.1
  2.4 0.9 copy-start.2
  3.3 0.8 copy-start.3
  4.1 0.8 copy-start.4

commit v2 on v1

v2 whole, which is shorter than its diff:
```python
import math

import jax
import jax.numpy as jnp
from jax import lax
from jax.experimental import pallas as pl
from jax.experimental.pallas import tpu as pltpu
from jax.sharding import PartitionSpec as P

D = 2048
TOKENS = 2560
ROWS = 80
LANES = 256
UNITS = 64
MESH = pl.DeviceIdType.MESH
F32 = jnp.float32
BF16 = jnp.bfloat16


def dot_nn(a, b):
    return lax.dot_general(a, b, (((1,), (0,)), ((), ())), preferred_element_type=F32)


def dot_nt(a, b):
    return lax.dot_general(a, b, (((1,), (1,)), ((), ())), preferred_element_type=F32)


def butterflies(parts):
    parts = list(parts)
    for bit in range(3):
        step = 1 << bit
        for low in range(8):
            if not low & step:
                a, b = parts[low], parts[low | step]
                parts[low], parts[low | step] = a + b, a - b
    return parts


def kernel(tok_hbm, og_hbm, gw, uw, dw, mixed, gtok, gg, gu, gd,
           WIN, TIN, AB, PK, WB, H, FS, WR, ROT, GACT, MP, R1, R2, ZS, ZR,
           WO, CS, CR, XS, X1, X2, ZW, ZWR, GTT,
           loads, zs, zr, zfs, zfr, zes, zer, ws, wr, ys, yr, y2s, y2r, xs, xr, cs, cr, os_, or_, os2, or2,
           es, er, gs, gr, vs, vr):
    dp = lax.axis_index("dp")
    te = lax.axis_index("tensor")
    x, zl, y = dp // 8, (dp // 4) % 2, dp % 4
    zh, c = te // 2, te % 2
    z = 2 * zh + zl
    k_own = te
    other = 1 - c
    home = c == zl
    xp, xm, xf = (x + 1) % 4, (x + 3) % 4, (x + 2) % 4
    yp, ym, yf = (y + 1) % 4, (y + 3) % 4, (y + 2) % 4

    def did(x_, y_, z_, c_):
        return ((x_ * 2 + z_ % 2) * 4 + y_, (z_ // 2) * 2 + c_)

    def rc(src, dst, send, recv, dev):
        return pltpu.make_async_remote_copy(
            src_ref=src, dst_ref=dst, send_sem=send, recv_sem=recv,
            device_id=dev, device_id_type=MESH)

    here = did(x, y, z, other)
    dev_x = (did(xp, y, z, c), did(xm, y, z, c), did(xf, y, z, c))
    dev_y = (did(x, yp, z, c), did(x, ym, z, c))
    sent, sent_home, sent_away = [], [], []

    def start(src, dst, send, recv, dev):
        cp = rc(src, dst, send, recv, dev)
        cp.start()
        sent.append(cp)

    def arrive(dst, recv):
        rc(dst, dst, recv, recv, here).wait_recv()

    barrier = pltpu.get_barrier_semaphore()

    def greet(dev):
        pl.semaphore_signal(barrier, inc=1, device_id=dev, device_id_type=MESH)

    for dz in range(8):
        for cc in range(2):
            if dz or cc:
                greet(did(x, y, (z + dz) % 8, (c + cc) % 2))
    for dev in dev_x + dev_y:
        greet(dev)

    fetched = [pltpu.make_async_copy(ref, WIN.at[n], loads.at[n]) for n, ref in enumerate((gw, uw, dw))]
    fetched_tokens = [pltpu.make_async_copy(ref, TIN.at[n], loads.at[3 + n]) for n, ref in enumerate((tok_hbm, og_hbm))]
    for cp in fetched_tokens + fetched:
        cp.start()
    tok, og = TIN.at[0], TIN.at[1]

    i = lax.broadcasted_iota(jnp.int32, (LANES, LANES), 0)
    j = lax.broadcasted_iota(jnp.int32, (LANES, LANES), 1)
    b = i & j
    b = b ^ (b >> 4)
    b = b ^ (b >> 2)
    b = (b ^ (b >> 1)) & 1
    H[...] = (1 - 2 * b).astype(F32).astype(BF16)

    for cp in fetched:
        cp.wait()
    gwt = WIN[0].astype(F32).T.astype(BF16)
    uwt = WIN[1].astype(F32).T.astype(BF16)
    for q in range(4):
        PK[q, 0:UNITS] = gwt[q * UNITS:(q + 1) * UNITS]
        PK[q, UNITS:2 * UNITS] = uwt[q * UNITS:(q + 1) * UNITS]
        PK[q, 2 * UNITS:3 * UNITS] = WIN[2, q * UNITS:(q + 1) * UNITS, :]
    WB[x, c, zh] = PK[zh]

    for cp in fetched_tokens:
        cp.wait()
    pl.semaphore_wait(barrier, 20)

    dev_z = (did(x, y, (z + 1) % 8, c), did(x, y, (z + 7) % 8, c))
    own_z = (did(x, y, (z + 1) % 8, zl), did(x, y, (z + 7) % 8, zl))
    away = jnp.logical_not(home)

    def send_tokens(a, ref):
        for way in range(2):
            start(ref, AB.at[a, y, k_own], zs.at[a, way], zr.at[a, k_own], own_z[way])

        cp = rc(ref, AB.at[a, y, k_own], zs.at[a, 2], zr.at[a, k_own], here)

        @pl.when(home)
        def _():
            pltpu.make_async_copy(ref, AB.at[a, y, k_own], zs.at[a, 2]).start()

        @pl.when(away)
        def _():
            cp.start()
        sent_away.append(cp)

    def send_weights(q):
        to = (zh + q) % 4
        start(PK.at[to], WB.at[x, c, zh], ws.at[q], wr.at[q], did(x, y, 2 * to + zl, c))

    shift = zl
    at_home = [zh, (zh + 3) % 4, (zh + 1) % 4, (zh + 2) % 4]
    at_away = [(zh + 3 + shift) % 4, (zh + shift) % 4, (zh + 2 + shift) % 4, (zh + 1 + shift) % 4]
    step_zh = [jnp.where(home, p, q) for p, q in zip(at_home, at_away)]

    def pair(a, yy, pos):
        return AB.at[a, yy, pl.ds(2 * step_zh[pos], 2)]

    def tokens_z(a, pos):
        near = step_zh[pos]
        one = [AB.at[a, y, 2 * near + n] for n in range(2)]
        both = pair(a, y, pos)
        sem = [zr.at[a, 2 * near + n] for n in range(2)]

        def relay(way):
            return rc(both, both, zfs.at[a, way], zfr.at[a, near], dev_z[way])

        def last(way):
            return rc(one[way], one[way], zes.at[a, way], zer.at[a, way], dev_z[way])

        if 0 < pos < 3:
            from_home = relay(pos - 1)
            sent_home.append(from_home)
        from_away = relay(pos) if pos < 2 else last(pos - 2)
        sent_away.append(from_away)

        @pl.when(home)
        def _():
            if pos == 0:
                arrive(AB.at[a, y, 2 * near + other], zr.at[a, 2 * near + other])
                pltpu.make_async_copy((tok, og)[a], AB.at[a, y, k_own], zs.at[a, 2]).wait()
            elif pos < 3:
                arrive(both, zfr.at[a, near])
                from_home.start()
            else:
                arrive(one[0], zer.at[a, 0])
                arrive(one[1], zer.at[a, 1])

        @pl.when(away)
        def _():
            if pos < 2:
                arrive(one[0], sem[0])
                arrive(one[1], sem[1])
                from_away.start()
            else:
                arrive(both, zfr.at[a, near])
                from_away.start()

    def tokens_out(a, pos):
        for way in range(2):
            start(pair(a, y, pos), pair(a, y, pos), ys.at[a, pos, way], yr.at[a, pos, way], dev_y[way])

    def weights_z(q):
        frm = (zh + 4 - q) % 4
        if q:
            arrive(WB.at[x, c, frm], wr.at[q])
        for way in range(3):
            start(WB.at[x, c, frm], WB.at[x, c, frm], xs.at[q, way], xr.at[q, way], dev_x[way])

    def tokens_y(a):
        for pos in range(4):
            for way in range(2):
                frm = (ym, yp)[way]
                arrive(pair(a, frm, pos), yr.at[a, pos, way])
                if (pos < 2) == (way == 0):
                    start(pair(a, frm, pos), pair(a, frm, pos), y2s.at[a, pos], y2r.at[a, pos], dev_y[way])

    def weights_x():
        start(WB.at[x, c], WB.at[x, c], cs.at[0], cr.at[0], here)
        for way in range(3):
            frm = (xm, xp, xf)[way]
            for q in (0, 1, 3, 2):
                arrive(WB.at[frm, c, (zh + 4 - q) % 4], xr.at[q, way])
            start(WB.at[frm, c], WB.at[frm, c], cs.at[1 + way], cr.at[1 + way], here)

    def weights_far():
        for n, frm in enumerate((x, xm, xp, xf)):
            arrive(WB.at[frm, other], cr.at[n])

    scale = 1.0 / math.sqrt(D)

    def spread(a, yy):
        def step(r, _):
            rows = pl.ds(pl.multiple_of(r * 16, 16), 16)
            parts = butterflies([FS[k, rows] for k in range(8)])
            for k in range(8):
                ROT[a, k, yy, rows] = (parts[k] * scale).astype(BF16)
            return 0
        lax.fori_loop(0, ROWS // 16, step, 0)

    def rotate_in(a, yy):
        FS[:, 0:ROWS] = dot_nn(AB[a, yy].reshape(8 * ROWS, LANES), H[...]).reshape(8, ROWS, LANES)
        spread(a, yy)

    def tokens_far(a):
        for pos in range(4):
            arrive(pair(a, yf, pos), y2r.at[a, pos])
        rotate_in(a, yf)

    send_tokens(0, tok)
    send_tokens(1, og)
    send_weights(1)
    send_weights(3)
    weights_z(0)
    for pos in range(2):
        for a in range(2):
            tokens_z(a, pos)
            tokens_out(a, pos)
    send_weights(2)
    weights_z(1)
    weights_z(3)
    for pos in range(2, 4):
        for a in range(2):
            tokens_z(a, pos)
            tokens_out(a, pos)
    weights_z(2)
    tokens_y(0)
    rotate_in(0, y)
    rotate_in(0, ym)
    tokens_y(1)
    rotate_in(0, yp)
    weights_x()
    tokens_far(0)
    weights_far()

    def rot(a, k):
        return ROT[a, k].reshape(4 * ROWS, LANES)

    def weight(w, k):
        return jnp.concatenate(
            [WB[q, k % 2, k // 2, w * UNITS:(w + 1) * UNITS] for q in range(4)], axis=0)

    def rotate_weight(w):
        for k in range(8):
            FS[k] = dot_nn(weight(w, k), H[...])

        def step(r, _):
            rows = pl.ds(pl.multiple_of(r * 16, 16), 16)
            parts = butterflies([FS[k, rows] for k in range(8)])
            for k in range(8):
                WR[w, k, rows] = (parts[k] * scale).astype(BF16)
            return 0
        lax.fori_loop(0, 256 // 16, step, 0)

    rot_tok = jnp.concatenate([rot(0, k) for k in range(8)], axis=1)

    def all_weight(w):
        return jnp.concatenate([weight(w, k) for k in range(8)], axis=1)

    gate = dot_nt(rot_tok, all_weight(0))
    up = dot_nt(rot_tok, all_weight(1))
    sigma = 1.0 / (1.0 + jnp.exp(-gate))
    hidden = (gate * sigma * up).astype(BF16)
    GTT[2] = hidden.astype(F32).T.astype(BF16)
    GACT[0] = up * sigma * (1.0 + gate * (1.0 - sigma))
    GACT[1] = gate * sigma

    def chunk(ref, n):
        return ref.at[pl.ds(2 * ((zh + n) % 4), 2)]

    def y_first(a, h):
        for n in (2 * h, 2 * h + 1):
            start(chunk(MP.at[a, yf], n), chunk(R1.at[a], n), os_.at[a, n], or_.at[a, n], dev_y[n % 2])
        for n in (2 * h, 2 * h + 1):
            frm = (ym, yp)[n % 2]
            start(chunk(MP.at[a, frm], n), chunk(R2.at[a, 1 - n % 2], n),
                  os_.at[a, 4 + n], or_.at[a, 4 + n], dev_y[1 - n % 2])

    def y_second(a, h):
        for n in (2 * h, 2 * h + 1):
            to = (yp, ym)[n % 2]
            arrive(chunk(R1.at[a], n), or_.at[a, n])
            ks = pl.ds(2 * ((zh + n) % 4), 2)
            MP[a, to, ks] = (MP[a, to, ks].astype(F32) + R1[a, ks].astype(F32)).astype(BF16)
            start(chunk(MP.at[a, to], n), chunk(R2.at[a, n % 2], n), os2.at[a, n], or2.at[a, n], dev_y[n % 2])

    def y_last(a, h):
        for n in (2 * h, 2 * h + 1):
            to = (zh + n) % 4
            ks = pl.ds(2 * to, 2)
            arrive(chunk(R2.at[a, 1 - n % 2], n), or_.at[a, 4 + n])
            arrive(chunk(R2.at[a, n % 2], n), or2.at[a, n])
            total = MP[a, y, ks].astype(F32) + R2[a, 0, ks].astype(F32) + R2[a, 1, ks].astype(F32)
            ZS[a, ks] = total.astype(BF16)
            for cc in (0, 1):
                to_c = (c + cc) % 2
                cp = rc(ZS.at[a, 2 * to + to_c], ZR.at[a, z], es.at[a, 2 * n + cc], er.at[a, z],
                        did(x, y, 2 * to + c, to_c))
                if n or cc:
                    cp.start()
                    sent.append(cp)
                else:
                    @pl.when(home)
                    def _():
                        ZR[a, z] = ZS[a, 2 * zh + c]

                    @pl.when(away)
                    def _():
                        cp.start()
                    sent_away.append(cp)

    def finish_tokens(a, out):
        for dz in range(8):
            frm = (z + dz) % 8
            if dz:
                arrive(ZR.at[a, frm], er.at[a, frm])
            else:
                @pl.when(jnp.logical_not(home))
                def _():
                    arrive(ZR.at[a, frm], er.at[a, frm])
        total = ZR[a, 0].astype(F32)
        for s in range(1, 8):
            total = total + ZR[a, s].astype(F32)
        out[...] = total

    def wgrads(w, parity, store):
        def step(q, _):
            g = dot_nn(GTT[w], ROT[w // 2, 2 * q + parity].reshape(4 * ROWS, LANES))
            for p in range(4):
                store(p, q, g[p * UNITS:(p + 1) * UNITS])
            return 0
        lax.fori_loop(0, 4, step, 0)

    def wgrads_other(w):
        def store(p, q, g):
            CS[w, p, q] = g.astype(BF16)
        wgrads(w, other, store)
        start(CS.at[w], CR.at[w], cs.at[4 + w], cr.at[4 + w], here)

    def wgrads_own(w):
        def store(p, q, g):
            WO[w, p, q] = g
        wgrads(w, c, store)

    lo, hi = pl.ds(0, 2), pl.ds(2, 2)

    def x_first(w):
        arrive(CR.at[w], cr.at[4 + w])
        XS[w, xf] = (WO[w, xf] + CR[w, xf].astype(F32)).astype(BF16)
        start(XS.at[w, xf, lo], X1.at[w, 0], gs.at[w, 0], gr.at[w, 0], dev_x[0])
        start(XS.at[w, xf, hi], X1.at[w, 1], gs.at[w, 1], gr.at[w, 1], dev_x[1])
        XS[w, xp, 2:4] = (WO[w, xp, 2:4] + CR[w, xp, 2:4].astype(F32)).astype(BF16)
        start(XS.at[w, xp, hi], X2.at[w, 0, hi], gs.at[w, 2], gr.at[w, 2], dev_x[0])
        XS[w, xm, 0:2] = (WO[w, xm, 0:2] + CR[w, xm, 0:2].astype(F32)).astype(BF16)
        start(XS.at[w, xm, lo], X2.at[w, 1, lo], gs.at[w, 3], gr.at[w, 3], dev_x[1])

    def x_second(w):
        arrive(X1.at[w, 0], gr.at[w, 0])
        XS[w, xp, 0:2] = (WO[w, xp, 0:2] + CR[w, xp, 0:2].astype(F32) + X1[w, 0].astype(F32)).astype(BF16)
        start(XS.at[w, xp, lo], X2.at[w, 0, lo], gs.at[w, 4], gr.at[w, 4], dev_x[0])
        arrive(X1.at[w, 1], gr.at[w, 1])
        XS[w, xm, 2:4] = (WO[w, xm, 2:4] + CR[w, xm, 2:4].astype(F32) + X1[w, 1].astype(F32)).astype(BF16)
        start(XS.at[w, xm, hi], X2.at[w, 1, hi], gs.at[w, 5], gr.at[w, 5], dev_x[1])

    factor = 1.0 / math.sqrt(TOKENS)

    def x_last(w):
        arrive(X2.at[w, 0, hi], gr.at[w, 2])
        arrive(X2.at[w, 1, lo], gr.at[w, 3])
        arrive(X2.at[w, 0, lo], gr.at[w, 4])
        arrive(X2.at[w, 1, hi], gr.at[w, 5])
        total = WO[w, x] + CR[w, x].astype(F32) + X2[w, 0].astype(F32) + X2[w, 1].astype(F32)
        ZW[w] = (total * factor).astype(BF16)
        for q in (1, 3, 2):
            to = (zh + q) % 4
            start(ZW.at[w, to], ZWR.at[w, zh], vs.at[w, q], vr.at[w, q], did(x, y, 2 * to + zl, c))
        ZWR[w, zh] = ZW[w, zh]

    def finish_grad(w, out):
        for q in (1, 3, 2):
            arrive(ZWR.at[w, (zh + 4 - q) % 4], vr.at[w, q])
        rows = ZWR[w].reshape(4 * UNITS, LANES)
        out[...] = rows if w == 2 else rows.astype(F32).T.astype(BF16)

    def partial(a, h, left, matrix):
        for n in (2 * h, 2 * h + 1):
            for e in range(2):
                k = 2 * ((zh + n) % 4) + e
                MP[a, :, k] = dot_nn(left, matrix(k)).astype(BF16).reshape(4, ROWS, LANES)
        y_first(a, h)

    rotate_weight(2)
    partial(0, 0, hidden, lambda k: WR[2, k])
    partial(0, 1, hidden, lambda k: WR[2, k])
    rotate_in(1, y)
    rotate_in(1, ym)
    rotate_in(1, yp)
    rotate_weight(0)
    y_second(0, 0)
    rotate_weight(1)
    y_second(0, 1)
    tokens_far(1)
    wgrads_other(2)

    rot_grad = jnp.concatenate([rot(1, k) for k in range(8)], axis=1)
    grad_hidden = dot_nt(rot_grad, all_weight(2))
    gga = grad_hidden * GACT[0]
    gua = grad_hidden * GACT[1]
    both = jnp.concatenate([gga.astype(BF16), gua.astype(BF16)], axis=1)

    def gate_up(k):
        return jnp.concatenate([WR[0, k], WR[1, k]], axis=0)

    partial(1, 0, both, gate_up)
    partial(1, 1, both, gate_up)
    wgrads_own(2)
    GTT[0] = gga.T.astype(BF16)
    wgrads_other(0)
    x_first(2)
    GTT[1] = gua.T.astype(BF16)
    wgrads_other(1)
    wgrads_own(0)
    x_first(0)
    x_second(2)
    y_last(0, 0)
    y_second(1, 0)
    wgrads_own(1)
    x_first(1)
    y_last(0, 1)
    y_second(1, 1)
    x_second(0)
    x_last(2)
    y_last(1, 0)
    x_second(1)
    x_last(0)
    y_last(1, 1)
    x_last(1)
    finish_tokens(0, mixed)
    finish_grad(2, gd)
    finish_grad(0, gg)
    finish_tokens(1, gtok)
    finish_grad(1, gu)

    for cp in sent:
        cp.wait_send()

    @pl.when(home)
    def _():
        for cp in sent_home:
            cp.wait_send()

    @pl.when(away)
    def _():
        for cp in sent_away:
            cp.wait_send()


def copies(*refs):
    n = 5
    ins, outs, held, sems = refs[:n], refs[n:2 * n], refs[2 * n:3 * n], refs[3 * n]
    loads = [pltpu.make_async_copy(ins[i], held[i], sems.at[0, i]) for i in range(n)]
    stores = [pltpu.make_async_copy(held[i], outs[i], sems.at[1, i]) for i in range(n)]
    for cp in loads:
        cp.start()
    for i in range(n):
        loads[i].wait()
        stores[i].start()
    for cp in stores:
        cp.wait()


def shards(tokens, gate_weight, up_weight, down_weight, out_grad):
    dma = pltpu.SemaphoreType.DMA
    vm = pltpu.VMEM
    block = jax.ShapeDtypeStruct
    rows, cols = tokens.shape
    outs = (
        block((ROWS, LANES), F32), block((ROWS, LANES), F32),
        block((256, 256), BF16), block((256, 256), BF16), block((256, 256), BF16))
    results = pl.pallas_call(
        kernel,
        out_shape=outs,
        in_specs=[pl.BlockSpec(memory_space=pl.ANY)] * 5,
        out_specs=[pl.BlockSpec(memory_space=vm)] * 5,
        scratch_shapes=[
            vm((3, 256, 256), BF16),
            vm((2, ROWS, LANES), BF16),
            vm((2, 4, 8, ROWS, LANES), BF16),
            vm((4, 192, LANES), BF16),
            vm((4, 2, 4, 192, LANES), BF16),
            vm((LANES, LANES), BF16),
            vm((8, 256, LANES), F32),
            vm((3, 8, 256, LANES), BF16),
            vm((2, 8, 4, ROWS, LANES), BF16),
            vm((2, 4 * ROWS, 256), F32),
            vm((2, 4, 8, ROWS, LANES), BF16),
            vm((2, 8, ROWS, LANES), BF16),
            vm((2, 2, 8, ROWS, LANES), BF16),
            vm((2, 8, ROWS, LANES), BF16),
            vm((2, 8, ROWS, LANES), BF16),
            vm((3, 4, 4, UNITS, LANES), F32),
            vm((3, 4, 4, UNITS, LANES), BF16),
            vm((3, 4, 4, UNITS, LANES), BF16),
            vm((3, 4, 4, UNITS, LANES), BF16),
            vm((3, 2, 2, UNITS, LANES), BF16),
            vm((3, 2, 4, UNITS, LANES), BF16),
            vm((3, 4, UNITS, LANES), BF16),
            vm((3, 4, UNITS, LANES), BF16),
            vm((3, 256, 4 * ROWS), BF16),
            dma((5,)), dma((2, 3)), dma((2, 8)), dma((2, 2)), dma((2, 4)), dma((2, 2)), dma((2, 2)),
            dma((4,)), dma((4,)),
            dma((2, 4, 2)), dma((2, 4, 2)), dma((2, 4)), dma((2, 4)),
            dma((4, 3)), dma((4, 3)),
            dma((8,)), dma((8,)), dma((2, 8)), dma((2, 8)), dma((2, 4)), dma((2, 4)),
            dma((2, 8)), dma((2, 8)), dma((3, 6)), dma((3, 6)), dma((3, 4)), dma((3, 4)),
        ],
        compiler_params=pltpu.CompilerParams(
            collective_id=0, has_side_effects=True, vmem_limit_bytes=56 << 20),
        name="layer",
    )(tokens, out_grad, gate_weight, up_weight, down_weight)
    return pl.pallas_call(
        copies,
        out_shape=outs,
        in_specs=[pl.BlockSpec(memory_space=pltpu.HBM)] * 5,
        out_specs=[pl.BlockSpec(memory_space=pltpu.HBM)] * 5,
        scratch_shapes=[vm(o.shape, o.dtype) for o in outs] + [dma((2, 5))],
        compiler_params=pltpu.CompilerParams(vmem_limit_bytes=60 << 20),
        name="results",
    )(*results)


def solution(mesh):
    return jax.shard_map(
        shards,
        mesh=mesh,
        in_specs=(P("dp", "tensor"), P("tensor", "dp"), P("tensor", "dp"), P("dp", "tensor"), P("dp", "tensor")),
        out_specs=(P("dp", "tensor"), P("dp", "tensor"), P("tensor", "dp"), P("tensor", "dp"), P("dp", "tensor")),
        check_vma=False,
    )
```

time: 102 us -> 89 us (0.87); the launches traced: 100 us -> 88.9 us
  local copies, waits for them, and re-layouts: 7.5 us -> 0 us
  Pallas kernels: 91.9 us -> 88.3 us
    unnamed x15 -> x0, local copies, waits for them, and re-layouts: 7.5 us -> none
    pallas_call x1 -> x2, Pallas kernels: 91.9 us -> 88.3 us  [the longest x1 86.4 us: shards(): pl.pallas_call(kernel, out_shape=outs, in_specs=[pl.BlockSpec(memory_spac...]
where the time goes in v2:
time: 89 us; the launch traced here: 88.9 us
  Pallas kernels  88.3 us (99%)
    pallas_call x1, Pallas kernels, shards(): pl.pallas_call(kernel, out_shape=outs, in_specs=[pl.BlockSpec(memory_spac...  86.4 us
    pallas_call x1, Pallas kernels, shards(): pl.pallas_call(copies, out_shape=outs, in_specs=[pl.BlockSpec(memory_spac...  1.85 us

profile of v2, /device:TPU:1, one launch (start us, length us, event | category | flops | bytes accessed | tf_op | source)
XLA Modules:
  0.0 88.9 jit_solution(3032598465272420949)
XLA Ops:
  0.6 86.4 %layer.1 = (f32[80,256]{1,0:T(8,128)}, f32[80,256]{1,0:T(8,128)}, bf16[256,256]{1,0:T(8,128)(2,1)}, bf16[256,256]{1,0:T(8,128)(2,1)}, bf16[256,256]{1,0:T(8,128)(2,1)}) custom-call(bf16[80,256]{1,0:T(8,128)(2,1)} %tok_hbm.1, bf16[80,256]{1,0:T(8,128)(2,1)} %og_hbm.1, bf16[256,256]{1,0:T(8,128)(2,1)} %gw.1, bf16[256,256]{1,0:T(8,128)(2,1)} %uw.1, ...), custom_call_target="tpu_custom_call" | custom-call | tf_op jit(solution)/shard_map/layer/pallas_call | solution.py:508
  87.0 1.9 %results.1 = (f32[80,256]{1,0:T(8,128)}, f32[80,256]{1,0:T(8,128)}, bf16[256,256]{1,0:T(8,128)(2,1)}, bf16[256,256]{1,0:T(8,128)(2,1)}, bf16[256,256]{1,0:T(8,128)(2,1)}) custom-call(f32[80,256]{1,0:T(8,128)} %get-tuple-element.10.refs_0_, f32[80,256]{1,0:T(8,128)} %get-tuple-element.11.refs_1_, bf16[256,256]{1,0:T(8,128)(2,1)} %get-tuple-element.12.refs_2_, ...), custom_call_target="tpu_custom_call" | custom-call | tf_op jit(solution)/shard_map/results/pallas_call | solution.py:549

commit v3 on v2

--- a/solution.py
+++ b/solution.py
@@ -37,10 +37,10 @@
 
 
 def kernel(tok_hbm, og_hbm, gw, uw, dw, mixed, gtok, gg, gu, gd,
-           WIN, TIN, AB, PK, WB, H, FS, WR, ROT, GACT, MP, R1, R2, ZS, ZR,
+           WIN, TIN, AB, PK, WB, H, FS, WR, ROT, GACT, MP, R1, R2, ZS, ZR, Q3, Q4, ZQ,
            WO, CS, CR, XS, X1, X2, ZW, ZWR, GTT,
            loads, zs, zr, zfs, zfr, zes, zer, ws, wr, ys, yr, y2s, y2r, xs, xr, cs, cr, os_, or_, os2, or2,
-           es, er, gs, gr, vs, vr):
+           es, er, q3s, q3r, q4s, q4r, gs, gr, vs, vr):
     dp = lax.axis_index("dp")
     te = lax.axis_index("tensor")
     x, zl, y = dp // 8, (dp // 4) % 2, dp % 4
@@ -91,27 +91,29 @@
         cp.start()
     tok, og = TIN.at[0], TIN.at[1]
 
-    i = lax.broadcasted_iota(jnp.int32, (LANES, LANES), 0)
-    j = lax.broadcasted_iota(jnp.int32, (LANES, LANES), 1)
-    b = i & j
-    b = b ^ (b >> 4)
-    b = b ^ (b >> 2)
-    b = (b ^ (b >> 1)) & 1
-    H[...] = (1 - 2 * b).astype(F32).astype(BF16)
-
-    for cp in fetched:
-        cp.wait()
-    gwt = WIN[0].astype(F32).T.astype(BF16)
-    uwt = WIN[1].astype(F32).T.astype(BF16)
-    for q in range(4):
-        PK[q, 0:UNITS] = gwt[q * UNITS:(q + 1) * UNITS]
-        PK[q, UNITS:2 * UNITS] = uwt[q * UNITS:(q + 1) * UNITS]
-        PK[q, 2 * UNITS:3 * UNITS] = WIN[2, q * UNITS:(q + 1) * UNITS, :]
-    WB[x, c, zh] = PK[zh]
-
     for cp in fetched_tokens:
         cp.wait()
     pl.semaphore_wait(barrier, 20)
+
+    def signs():
+        i = lax.broadcasted_iota(jnp.int32, (LANES, LANES), 0)
+        j = lax.broadcasted_iota(jnp.int32, (LANES, LANES), 1)
+        b = i & j
+        b = b ^ (b >> 4)
+        b = b ^ (b >> 2)
+        b = (b ^ (b >> 1)) & 1
+        H[...] = (1 - 2 * b).astype(F32).astype(BF16)
+
+    def pack():
+        for cp in fetched:
+            cp.wait()
+        gwt = WIN[0].astype(F32).T.astype(BF16)
+        uwt = WIN[1].astype(F32).T.astype(BF16)
+        for q in range(4):
+            PK[q, 0:UNITS] = gwt[q * UNITS:(q + 1) * UNITS]
+            PK[q, UNITS:2 * UNITS] = uwt[q * UNITS:(q + 1) * UNITS]
+            PK[q, 2 * UNITS:3 * UNITS] = WIN[2, q * UNITS:(q + 1) * UNITS, :]
+        WB[x, c, zh] = PK[zh]
 
     dev_z = (did(x, y, (z + 1) % 8, c), did(x, y, (z + 7) % 8, c))
     own_z = (did(x, y, (z + 1) % 8, zl), did(x, y, (z + 7) % 8, zl))
@@ -195,21 +197,20 @@
         for way in range(3):
             start(WB.at[x, c, frm], WB.at[x, c, frm], xs.at[q, way], xr.at[q, way], dev_x[way])
 
-    def tokens_y(a):
-        for pos in range(4):
+    def to_core(n):
+        frm = (x, xm, xp, xf)[n]
+        if n:
+            for q in range(4):
+                arrive(WB.at[frm, c, (zh + 4 - q) % 4], xr.at[q, n - 1])
+        start(WB.at[frm, c], WB.at[frm, c], cs.at[n], cr.at[n], here)
+
+    def tokens_y(a, steps=range(4)):
+        for pos in steps:
             for way in range(2):
                 frm = (ym, yp)[way]
                 arrive(pair(a, frm, pos), yr.at[a, pos, way])
                 if (pos < 2) == (way == 0):
                     start(pair(a, frm, pos), pair(a, frm, pos), y2s.at[a, pos], y2r.at[a, pos], dev_y[way])
-
-    def weights_x():
-        start(WB.at[x, c], WB.at[x, c], cs.at[0], cr.at[0], here)
-        for way in range(3):
-            frm = (xm, xp, xf)[way]
-            for q in (0, 1, 3, 2):
-                arrive(WB.at[frm, c, (zh + 4 - q) % 4], xr.at[q, way])
-            start(WB.at[frm, c], WB.at[frm, c], cs.at[1 + way], cr.at[1 + way], here)
 
     def weights_far():
         for n, frm in enumerate((x, xm, xp, xf)):
@@ -235,31 +236,6 @@
             arrive(pair(a, yf, pos), y2r.at[a, pos])
         rotate_in(a, yf)
 
-    send_tokens(0, tok)
-    send_tokens(1, og)
-    send_weights(1)
-    send_weights(3)
-    weights_z(0)
-    for pos in range(2):
-        for a in range(2):
-            tokens_z(a, pos)
-            tokens_out(a, pos)
-    send_weights(2)
-    weights_z(1)
-    weights_z(3)
-    for pos in range(2, 4):
-        for a in range(2):
-            tokens_z(a, pos)
-            tokens_out(a, pos)
-    weights_z(2)
-    tokens_y(0)
-    rotate_in(0, y)
-    rotate_in(0, ym)
-    tokens_y(1)
-    rotate_in(0, yp)
-    weights_x()
-    tokens_far(0)
-    weights_far()
 
     def rot(a, k):
         return ROT[a, k].reshape(4 * ROWS, LANES)
@@ -280,18 +256,41 @@
             return 0
         lax.fori_loop(0, 256 // 16, step, 0)
 
-    rot_tok = jnp.concatenate([rot(0, k) for k in range(8)], axis=1)
-
     def all_weight(w):
         return jnp.concatenate([weight(w, k) for k in range(8)], axis=1)
 
-    gate = dot_nt(rot_tok, all_weight(0))
-    up = dot_nt(rot_tok, all_weight(1))
-    sigma = 1.0 / (1.0 + jnp.exp(-gate))
-    hidden = (gate * sigma * up).astype(BF16)
-    GTT[2] = hidden.astype(F32).T.astype(BF16)
-    GACT[0] = up * sigma * (1.0 + gate * (1.0 - sigma))
-    GACT[1] = gate * sigma
+    def all_rot(a):
+        return jnp.concatenate([rot(a, k) for k in range(8)], axis=1)
+
+    kept = {}
+
+    def gates():
+        tokens = all_rot(0)
+        gate = dot_nt(tokens, all_weight(0))
+        up = dot_nt(tokens, all_weight(1))
+        sigma = 1.0 / (1.0 + jnp.exp(-gate))
+        hidden = gate * sigma * up
+        kept[0] = hidden.astype(BF16)
+        GTT[2] = hidden.T.astype(BF16)
+        GACT[0] = up * sigma * (1.0 + gate * (1.0 - sigma))
+        GACT[1] = gate * sigma
+
+    def hidden_grads():
+        grad_hidden = dot_nt(all_rot(1), all_weight(2))
+        kept["gate"] = grad_hidden * GACT[0]
+        kept["up"] = grad_hidden * GACT[1]
+        kept[1] = jnp.concatenate([kept["gate"].astype(BF16), kept["up"].astype(BF16)], axis=1)
+
+    def turn(w):
+        GTT[w] = kept[("gate", "up")[w]].T.astype(BF16)
+
+    def partial(a, h):
+        for n in (2 * h, 2 * h + 1):
+            for e in range(2):
+                k = 2 * ((zh + n) % 4) + e
+                matrix = jnp.concatenate([WR[0, k], WR[1, k]], axis=0) if a else WR[2, k]
+                MP[a, :, k] = dot_nn(kept[a], matrix).astype(BF16).reshape(4, ROWS, LANES)
+        y_first(a, h)
 
     def chunk(ref, n):
         return ref.at[pl.ds(2 * ((zh + n) % 4), 2)]
@@ -312,43 +311,69 @@
             MP[a, to, ks] = (MP[a, to, ks].astype(F32) + R1[a, ks].astype(F32)).astype(BF16)
             start(chunk(MP.at[a, to], n), chunk(R2.at[a, n % 2], n), os2.at[a, n], or2.at[a, n], dev_y[n % 2])
 
-    def y_last(a, h):
-        for n in (2 * h, 2 * h + 1):
-            to = (zh + n) % 4
-            ks = pl.ds(2 * to, 2)
+    def near_z(n):
+        return did(x, y, (z + n) % 8, c)
+
+    def owner(n, cc):
+        return did(x, y, (z + n) % 8, cc)
+
+    def to_zh(n):
+        return (zh + n) % 4
+
+    def y_last(a):
+        for n in range(4):
+            ks = pl.ds(2 * to_zh(n), 2)
             arrive(chunk(R2.at[a, 1 - n % 2], n), or_.at[a, 4 + n])
             arrive(chunk(R2.at[a, n % 2], n), or2.at[a, n])
             total = MP[a, y, ks].astype(F32) + R2[a, 0, ks].astype(F32) + R2[a, 1, ks].astype(F32)
             ZS[a, ks] = total.astype(BF16)
-            for cc in (0, 1):
-                to_c = (c + cc) % 2
-                cp = rc(ZS.at[a, 2 * to + to_c], ZR.at[a, z], es.at[a, 2 * n + cc], er.at[a, z],
-                        did(x, y, 2 * to + c, to_c))
-                if n or cc:
-                    cp.start()
-                    sent.append(cp)
-                else:
-                    @pl.when(home)
-                    def _():
-                        ZR[a, z] = ZS[a, 2 * zh + c]
-
-                    @pl.when(away)
-                    def _():
-                        cp.start()
-                    sent_away.append(cp)
+        far = [rc(ZS.at[a, 2 * to_zh(2) + w], Q4.at[a, w], q4s.at[a, w], q4r.at[a, w], near_z((2, 6)[w]))
+               for w in range(2)]
+        own = rc(ZS.at[a, 2 * zh + other], ZR.at[a, 0], es.at[a, 0], er.at[a, 0], here)
+        thirds = [rc(ZS.at[a, pl.ds(2 * to_zh((1, 2)[w] + zl), 2)], Q3.at[a, w], q3s.at[a, w], q3r.at[a, w],
+                     near_z((1, 7)[w])) for w in range(2)]
+        firsts = [rc(ZS.at[a, 2 * to_zh((0, 3)[w] + zl) + cc], ZR.at[a, 1 + w], es.at[a, 1 + 2 * w + cc],
+                     er.at[a, 1 + w], owner((1, 7)[w], cc)) for w in range(2) for cc in range(2)]
+        sent_home.extend(far + [own])
+        sent_away.extend(thirds + firsts)
+
+        @pl.when(home)
+        def _():
+            for cp in far:
+                cp.start()
+            own.start()
+            ZR[a, 0] = ZS[a, 2 * zh + c]
+
+        @pl.when(away)
+        def _():
+            for cp in thirds + firsts:
+                cp.start()
+
+    def z_second(a):
+        seconds = [rc(ZQ.at[a, w, cc], ZR.at[a, 3 + w], es.at[a, 5 + 2 * w + cc], er.at[a, 3 + w],
+                      owner((2, 6)[w], cc)) for w in range(2) for cc in range(2)]
+        sent_home.extend(seconds)
+
+        @pl.when(home)
+        def _():
+            for w in range(2):
+                arrive(Q3.at[a, w], q3r.at[a, w])
+                arrive(Q4.at[a, w], q4r.at[a, w])
+                for cc in range(2):
+                    total = ZS[a, 2 * to_zh((1, 3)[w]) + cc].astype(F32) + Q3[a, w, cc].astype(F32)
+                    if cc == w:
+                        total = total + Q4[a, w].astype(F32)
+                    ZQ[a, w, cc] = total.astype(BF16)
+                    seconds[2 * w + cc].start()
 
     def finish_tokens(a, out):
-        for dz in range(8):
-            frm = (z + dz) % 8
-            if dz:
-                arrive(ZR.at[a, frm], er.at[a, frm])
-            else:
-                @pl.when(jnp.logical_not(home))
-                def _():
-                    arrive(ZR.at[a, frm], er.at[a, frm])
+        @pl.when(away)
+        def _():
+            arrive(ZR.at[a, 0], er.at[a, 0])
         total = ZR[a, 0].astype(F32)
-        for s in range(1, 8):
-            total = total + ZR[a, s].astype(F32)
+        for n in range(1, 5):
+            arrive(ZR.at[a, n], er.at[a, n])
+            total = total + ZR[a, n].astype(F32)
         out[...] = total
 
     def wgrads(w, parity, store):
@@ -410,64 +435,93 @@
         rows = ZWR[w].reshape(4 * UNITS, LANES)
         out[...] = rows if w == 2 else rows.astype(F32).T.astype(BF16)
 
-    def partial(a, h, left, matrix):
-        for n in (2 * h, 2 * h + 1):
-            for e in range(2):
-                k = 2 * ((zh + n) % 4) + e
-                MP[a, :, k] = dot_nn(left, matrix(k)).astype(BF16).reshape(4, ROWS, LANES)
-        y_first(a, h)
-
+    send_tokens(0, tok)
+    send_tokens(1, og)
+    pack()
+    send_weights(1)
+    send_weights(3)
+    weights_z(0)
+    signs()
+    tokens_z(0, 0)
+    tokens_out(0, 0)
+    tokens_z(1, 0)
+    tokens_out(1, 0)
+    tokens_z(0, 1)
+    tokens_out(0, 1)
+    tokens_z(1, 1)
+    tokens_out(1, 1)
+    send_weights(2)
+    weights_z(1)
+    weights_z(3)
+    tokens_z(0, 2)
+    tokens_out(0, 2)
+    tokens_z(1, 2)
+    tokens_out(1, 2)
+    tokens_z(0, 3)
+    tokens_out(0, 3)
+    tokens_z(1, 3)
+    tokens_out(1, 3)
+    weights_z(2)
+    tokens_y(0, (0,))
+    tokens_y(0, (1,))
+    tokens_y(0, (2,))
+    tokens_y(0, (3,))
+    rotate_in(0, y)
+    rotate_in(0, ym)
+    tokens_y(1, (0,))
+    tokens_y(1, (1,))
+    tokens_y(1, (2,))
+    tokens_y(1, (3,))
+    rotate_in(0, yp)
+    to_core(0)
+    to_core(1)
+    to_core(2)
+    to_core(3)
+    tokens_far(0)
+    weights_far()
+    gates()
     rotate_weight(2)
-    partial(0, 0, hidden, lambda k: WR[2, k])
-    partial(0, 1, hidden, lambda k: WR[2, k])
+    partial(0, 0)
+    partial(0, 1)
     rotate_in(1, y)
     rotate_in(1, ym)
     rotate_in(1, yp)
     rotate_weight(0)
-    y_second(0, 0)
     rotate_weight(1)
-    y_second(0, 1)
     tokens_far(1)
     wgrads_other(2)
-
-    rot_grad = jnp.concatenate([rot(1, k) for k in range(8)], axis=1)
-    grad_hidden = dot_nt(rot_grad, all_weight(2))
-    gga = grad_hidden * GACT[0]
-    gua = grad_hidden * GACT[1]
-    both = jnp.concatenate([gga.astype(BF16), gua.astype(BF16)], axis=1)
-
-    def gate_up(k):
-        return jnp.concatenate([WR[0, k], WR[1, k]], axis=0)
-
-    partial(1, 0, both, gate_up)
-    partial(1, 1, both, gate_up)
+    hidden_grads()
+    y_second(0, 0)
+    y_second(0, 1)
+    partial(1, 0)
+    partial(1, 1)
     wgrads_own(2)
-    GTT[0] = gga.T.astype(BF16)
+    x_first(2)
+    turn(0)
     wgrads_other(0)
-    x_first(2)
-    GTT[1] = gua.T.astype(BF16)
+    wgrads_own(0)
+    x_second(2)
+    y_last(0)
+    turn(1)
     wgrads_other(1)
-    wgrads_own(0)
     x_first(0)
-    x_second(2)
-    y_last(0, 0)
+    wgrads_own(1)
+    x_last(2)
+    z_second(0)
     y_second(1, 0)
-    wgrads_own(1)
+    y_second(1, 1)
     x_first(1)
-    y_last(0, 1)
-    y_second(1, 1)
     x_second(0)
-    x_last(2)
-    y_last(1, 0)
+    x_last(0)
     x_second(1)
-    x_last(0)
-    y_last(1, 1)
+    y_last(1)
     x_last(1)
     finish_tokens(0, mixed)
     finish_grad(2, gd)
+    z_second(1)
     finish_grad(0, gg)
+    finish_grad(1, gu)
     finish_tokens(1, gtok)
-    finish_grad(1, gu)
 
     for cp in sent:
         cp.wait_send()
@@ -525,7 +579,10 @@
             vm((2, 8, ROWS, LANES), BF16),
             vm((2, 2, 8, ROWS, LANES), BF16),
             vm((2, 8, ROWS, LANES), BF16),
-            vm((2, 8, ROWS, LANES), BF16),
+            vm((2, 5, ROWS, LANES), BF16),
+            vm((2, 2, 2, ROWS, LANES), BF16),
+            vm((2, 2, ROWS, LANES), BF16),
+            vm((2, 2, 2, ROWS, LANES), BF16),
             vm((3, 4, 4, UNITS, LANES), F32),
             vm((3, 4, 4, UNITS, LANES), BF16),
             vm((3, 4, 4, UNITS, LANES), BF16),
@@ -540,7 +597,7 @@
             dma((2, 4, 2)), dma((2, 4, 2)), dma((2, 4)), dma((2, 4)),
             dma((4, 3)), dma((4, 3)),
             dma((8,)), dma((8,)), dma((2, 8)), dma((2, 8)), dma((2, 4)), dma((2, 4)),
-            dma((2, 8)), dma((2, 8)), dma((3, 6)), dma((3, 6)), dma((3, 4)), dma((3, 4)),
+            dma((2, 9)), dma((2, 5)), dma((2, 2)), dma((2, 2)), dma((2, 2)), dma((2, 2)), dma((3, 6)), dma((3, 6)), dma((3, 4)), dma((3, 4)),
         ],
         compiler_params=pltpu.CompilerParams(
             collective_id=0, has_side_effects=True, vmem_limit_bytes=56 << 20),

time: 89 us -> 82.9 us (0.931)
  Pallas kernels: 88.3 us -> 82.1 us
    pallas_call x1, Pallas kernels: 86.4 us -> 80.3 us  [shards(): pl.pallas_call(kernel, out_shape=outs, in_specs=[pl.BlockSpec(memory_spac...]
where the time goes in v3:
time: 82.9 us; the launch traced here: 82.8 us
  Pallas kernels  82.1 us (99%)
    pallas_call x1, Pallas kernels, shards(): pl.pallas_call(kernel, out_shape=outs, in_specs=[pl.BlockSpec(memory_spac...  80.3 us
    pallas_call x1, Pallas kernels, shards(): pl.pallas_call(copies, out_shape=outs, in_specs=[pl.BlockSpec(memory_spac...  1.85 us

profile of v3, /device:TPU:1, one launch (start us, length us, event | category | flops | bytes accessed | tf_op | source)
XLA Modules:
  0.0 82.8 jit_solution(2237554440741080237)
XLA Ops:
  0.6 80.3 %layer.1 = (f32[80,256]{1,0:T(8,128)}, f32[80,256]{1,0:T(8,128)}, bf16[256,256]{1,0:T(8,128)(2,1)}, bf16[256,256]{1,0:T(8,128)(2,1)}, bf16[256,256]{1,0:T(8,128)(2,1)}) custom-call(bf16[80,256]{1,0:T(8,128)(2,1)} %tok_hbm.1, bf16[80,256]{1,0:T(8,128)(2,1)} %og_hbm.1, bf16[256,256]{1,0:T(8,128)(2,1)} %gw.1, bf16[256,256]{1,0:T(8,128)(2,1)} %uw.1, ...), custom_call_target="tpu_custom_call" | custom-call | tf_op jit(solution)/shard_map/layer/pallas_call | solution.py:562
  80.9 1.9 %results.1 = (f32[80,256]{1,0:T(8,128)}, f32[80,256]{1,0:T(8,128)}, bf16[256,256]{1,0:T(8,128)(2,1)}, bf16[256,256]{1,0:T(8,128)(2,1)}, bf16[256,256]{1,0:T(8,128)(2,1)}) custom-call(f32[80,256]{1,0:T(8,128)} %get-tuple-element.10.refs_0_, f32[80,256]{1,0:T(8,128)} %get-tuple-element.11.refs_1_, bf16[256,256]{1,0:T(8,128)(2,1)} %get-tuple-element.12.refs_2_, ...), custom_call_target="tpu_custom_call" | custom-call | tf_op jit(solution)/shard_map/results/pallas_call | solution.py:606

commit v4 on v3

--- a/solution.py
+++ b/solution.py
@@ -38,9 +38,9 @@
 
 def kernel(tok_hbm, og_hbm, gw, uw, dw, mixed, gtok, gg, gu, gd,
            WIN, TIN, AB, PK, WB, H, FS, WR, ROT, GACT, MP, R1, R2, ZS, ZR, Q3, Q4, ZQ,
-           WO, CS, CR, XS, X1, X2, ZW, ZWR, GTT,
+           WO, CS, CR, XS, X2, ZW, ZWR, GTT,
            loads, zs, zr, zfs, zfr, zes, zer, ws, wr, ys, yr, y2s, y2r, xs, xr, cs, cr, os_, or_, os2, or2,
-           es, er, q3s, q3r, q4s, q4r, gs, gr, vs, vr):
+           TOUT, GOUT, outs, es, er, q3s, q3r, q4s, q4r, gs, gr, vs, vr):
     dp = lax.axis_index("dp")
     te = lax.axis_index("tensor")
     x, zl, y = dp // 8, (dp // 4) % 2, dp % 4
@@ -69,6 +69,13 @@
         cp = rc(src, dst, send, recv, dev)
         cp.start()
         sent.append(cp)
+
+    leaving = []
+
+    def leave(src, dst, n):
+        cp = pltpu.make_async_copy(src, dst, outs.at[n])
+        cp.start()
+        leaving.append(cp)
 
     def arrive(dst, recv):
         rc(dst, dst, recv, recv, here).wait_recv()
@@ -374,7 +381,8 @@
         for n in range(1, 5):
             arrive(ZR.at[a, n], er.at[a, n])
             total = total + ZR[a, n].astype(F32)
-        out[...] = total
+        TOUT[a] = total
+        leave(TOUT.at[a], out, a)
 
     def wgrads(w, parity, store):
         def step(q, _):
@@ -395,34 +403,19 @@
             WO[w, p, q] = g
         wgrads(w, c, store)
 
-    lo, hi = pl.ds(0, 2), pl.ds(2, 2)
-
     def x_first(w):
         arrive(CR.at[w], cr.at[4 + w])
-        XS[w, xf] = (WO[w, xf] + CR[w, xf].astype(F32)).astype(BF16)
-        start(XS.at[w, xf, lo], X1.at[w, 0], gs.at[w, 0], gr.at[w, 0], dev_x[0])
-        start(XS.at[w, xf, hi], X1.at[w, 1], gs.at[w, 1], gr.at[w, 1], dev_x[1])
-        XS[w, xp, 2:4] = (WO[w, xp, 2:4] + CR[w, xp, 2:4].astype(F32)).astype(BF16)
-        start(XS.at[w, xp, hi], X2.at[w, 0, hi], gs.at[w, 2], gr.at[w, 2], dev_x[0])
-        XS[w, xm, 0:2] = (WO[w, xm, 0:2] + CR[w, xm, 0:2].astype(F32)).astype(BF16)
-        start(XS.at[w, xm, lo], X2.at[w, 1, lo], gs.at[w, 3], gr.at[w, 3], dev_x[1])
-
-    def x_second(w):
-        arrive(X1.at[w, 0], gr.at[w, 0])
-        XS[w, xp, 0:2] = (WO[w, xp, 0:2] + CR[w, xp, 0:2].astype(F32) + X1[w, 0].astype(F32)).astype(BF16)
-        start(XS.at[w, xp, lo], X2.at[w, 0, lo], gs.at[w, 4], gr.at[w, 4], dev_x[0])
-        arrive(X1.at[w, 1], gr.at[w, 1])
-        XS[w, xm, 2:4] = (WO[w, xm, 2:4] + CR[w, xm, 2:4].astype(F32) + X1[w, 1].astype(F32)).astype(BF16)
-        start(XS.at[w, xm, hi], X2.at[w, 1, hi], gs.at[w, 5], gr.at[w, 5], dev_x[1])
+        for n, to in enumerate((xp, xm, xf)):
+            XS[w, to] = (WO[w, to] + CR[w, to].astype(F32)).astype(BF16)
+            start(XS.at[w, to], X2.at[w, n], gs.at[w, n], gr.at[w, n], dev_x[n])
 
     factor = 1.0 / math.sqrt(TOKENS)
 
     def x_last(w):
-        arrive(X2.at[w, 0, hi], gr.at[w, 2])
-        arrive(X2.at[w, 1, lo], gr.at[w, 3])
-        arrive(X2.at[w, 0, lo], gr.at[w, 4])
-        arrive(X2.at[w, 1, hi], gr.at[w, 5])
-        total = WO[w, x] + CR[w, x].astype(F32) + X2[w, 0].astype(F32) + X2[w, 1].astype(F32)
+        total = WO[w, x] + CR[w, x].astype(F32)
+        for n in range(3):
+            arrive(X2.at[w, n], gr.at[w, n])
+            total = total + X2[w, n].astype(F32)
         ZW[w] = (total * factor).astype(BF16)
         for q in (1, 3, 2):
             to = (zh + q) % 4
@@ -433,7 +426,8 @@
         for q in (1, 3, 2):
             arrive(ZWR.at[w, (zh + 4 - q) % 4], vr.at[w, q])
         rows = ZWR[w].reshape(4 * UNITS, LANES)
-        out[...] = rows if w == 2 else rows.astype(F32).T.astype(BF16)
+        GOUT[w] = rows if w == 2 else rows.astype(F32).T.astype(BF16)
+        leave(GOUT.at[w], out, 2 + w)
 
     send_tokens(0, tok)
     send_tokens(1, og)
@@ -500,20 +494,17 @@
     turn(0)
     wgrads_other(0)
     wgrads_own(0)
-    x_second(2)
     y_last(0)
     turn(1)
     wgrads_other(1)
     x_first(0)
     wgrads_own(1)
-    x_last(2)
+    x_first(1)
     z_second(0)
     y_second(1, 0)
     y_second(1, 1)
-    x_first(1)
-    x_second(0)
+    x_last(2)
     x_last(0)
-    x_second(1)
     y_last(1)
     x_last(1)
     finish_tokens(0, mixed)
@@ -525,6 +516,8 @@
 
     for cp in sent:
         cp.wait_send()
+    for cp in leaving:
+        cp.wait()
 
     @pl.when(home)
     def _():
@@ -563,7 +556,7 @@
         kernel,
         out_shape=outs,
         in_specs=[pl.BlockSpec(memory_space=pl.ANY)] * 5,
-        out_specs=[pl.BlockSpec(memory_space=vm)] * 5,
+        out_specs=[pl.BlockSpec(memory_space=pltpu.HBM)] * 5,
         scratch_shapes=[
             vm((3, 256, 256), BF16),
             vm((2, ROWS, LANES), BF16),
@@ -587,8 +580,7 @@
             vm((3, 4, 4, UNITS, LANES), BF16),
             vm((3, 4, 4, UNITS, LANES), BF16),
             vm((3, 4, 4, UNITS, LANES), BF16),
-            vm((3, 2, 2, UNITS, LANES), BF16),
-            vm((3, 2, 4, UNITS, LANES), BF16),
+            vm((3, 3, 4, UNITS, LANES), BF16),
             vm((3, 4, UNITS, LANES), BF16),
             vm((3, 4, UNITS, LANES), BF16),
             vm((3, 256, 4 * ROWS), BF16),
@@ -597,7 +589,8 @@
             dma((2, 4, 2)), dma((2, 4, 2)), dma((2, 4)), dma((2, 4)),
             dma((4, 3)), dma((4, 3)),
             dma((8,)), dma((8,)), dma((2, 8)), dma((2, 8)), dma((2, 4)), dma((2, 4)),
-            dma((2, 9)), dma((2, 5)), dma((2, 2)), dma((2, 2)), dma((2, 2)), dma((2, 2)), dma((3, 6)), dma((3, 6)), dma((3, 4)), dma((3, 4)),
+            vm((2, ROWS, LANES), F32), vm((3, 256, 256), BF16), dma((5,)),
+            dma((2, 9)), dma((2, 5)), dma((2, 2)), dma((2, 2)), dma((2, 2)), dma((2, 2)), dma((3, 3)), dma((3, 3)), dma((3, 4)), dma((3, 4)),
         ],
         compiler_params=pltpu.CompilerParams(
             collective_id=0, has_side_effects=True, vmem_limit_bytes=56 << 20),

time: 82.9 us -> 82.1 us (level)
  no operation moved by 1% of the time
where the time goes in v4:
time: 82.1 us; the launch traced here: 82 us
  Pallas kernels  81.4 us (99%)
    pallas_call x1, Pallas kernels, shards(): pl.pallas_call(kernel, out_shape=outs, in_specs=[pl.BlockSpec(memory_spac...  79.5 us
    pallas_call x1, Pallas kernels, shards(): pl.pallas_call(copies, out_shape=outs, in_specs=[pl.BlockSpec(memory_spac...  1.85 us

profile of v4, /device:TPU:1, one launch (start us, length us, event | category | flops | bytes accessed | tf_op | source)
XLA Modules:
  0.0 82.0 jit_solution(10150621872476230867)
XLA Ops:
  0.6 79.5 %layer.1 = (f32[80,256]{1,0:T(8,128)}, f32[80,256]{1,0:T(8,128)}, bf16[256,256]{1,0:T(8,128)(2,1)}, bf16[256,256]{1,0:T(8,128)(2,1)}, bf16[256,256]{1,0:T(8,128)(2,1)}) custom-call(bf16[80,256]{1,0:T(8,128)(2,1)} %tok_hbm.1, bf16[80,256]{1,0:T(8,128)(2,1)} %og_hbm.1, bf16[256,256]{1,0:T(8,128)(2,1)} %gw.1, bf16[256,256]{1,0:T(8,128)(2,1)} %uw.1, ...), custom_call_target="tpu_custom_call" | custom-call | tf_op jit(solution)/shard_map/layer/pallas_call | solution.py:555
  80.2 1.9 %results.1 = (f32[80,256]{1,0:T(8,128)}, f32[80,256]{1,0:T(8,128)}, bf16[256,256]{1,0:T(8,128)(2,1)}, bf16[256,256]{1,0:T(8,128)(2,1)}, bf16[256,256]{1,0:T(8,128)(2,1)}) custom-call(f32[80,256]{1,0:T(8,128)} %get-tuple-element.10.refs_0_, f32[80,256]{1,0:T(8,128)} %get-tuple-element.11.refs_1_, bf16[256,256]{1,0:T(8,128)(2,1)} %get-tuple-element.12.refs_2_, ...), custom_call_target="tpu_custom_call" | custom-call | tf_op jit(solution)/shard_map/results/pallas_call | solution.py:599

commit v5 on v4

--- a/solution.py
+++ b/solution.py
@@ -489,6 +489,7 @@
     y_second(0, 1)
     partial(1, 0)
     partial(1, 1)
+    early = len(sent)
     wgrads_own(2)
     x_first(2)
     turn(0)
@@ -505,6 +506,8 @@
     y_second(1, 1)
     x_last(2)
     x_last(0)
+    for cp in sent[:early]:
+        cp.wait_send()
     y_last(1)
     x_last(1)
     finish_tokens(0, mixed)
@@ -514,7 +517,7 @@
     finish_grad(1, gu)
     finish_tokens(1, gtok)
 
-    for cp in sent:
+    for cp in sent[early:]:
         cp.wait_send()
     for cp in leaving:
         cp.wait()

time: 82.1 us -> 82.1 us (level)
  no operation moved by 1% of the time
where the time goes in v5:
time: 82.1 us; the launch traced here: 82 us
  Pallas kernels  81.4 us (99%)
    pallas_call x1, Pallas kernels, shards(): pl.pallas_call(kernel, out_shape=outs, in_specs=[pl.BlockSpec(memory_spac...  79.5 us
    pallas_call x1, Pallas kernels, shards(): pl.pallas_call(copies, out_shape=outs, in_specs=[pl.BlockSpec(memory_spac...  1.85 us

profile of v5, /device:TPU:1, one launch (start us, length us, event | category | flops | bytes accessed | tf_op | source)
XLA Modules:
  0.0 82.0 jit_solution(4278142533219320076)
XLA Ops:
  0.6 79.5 %layer.1 = (f32[80,256]{1,0:T(8,128)}, f32[80,256]{1,0:T(8,128)}, bf16[256,256]{1,0:T(8,128)(2,1)}, bf16[256,256]{1,0:T(8,128)(2,1)}, bf16[256,256]{1,0:T(8,128)(2,1)}) custom-call(bf16[80,256]{1,0:T(8,128)(2,1)} %tok_hbm.1, bf16[80,256]{1,0:T(8,128)(2,1)} %og_hbm.1, bf16[256,256]{1,0:T(8,128)(2,1)} %gw.1, bf16[256,256]{1,0:T(8,128)(2,1)} %uw.1, ...), custom_call_target="tpu_custom_call" | custom-call | tf_op jit(solution)/shard_map/layer/pallas_call | solution.py:558
  80.2 1.9 %results.1 = (f32[80,256]{1,0:T(8,128)}, f32[80,256]{1,0:T(8,128)}, bf16[256,256]{1,0:T(8,128)(2,1)}, bf16[256,256]{1,0:T(8,128)(2,1)}, bf16[256,256]{1,0:T(8,128)(2,1)}) custom-call(f32[80,256]{1,0:T(8,128)} %get-tuple-element.10.refs_0_, f32[80,256]{1,0:T(8,128)} %get-tuple-element.11.refs_1_, bf16[256,256]{1,0:T(8,128)(2,1)} %get-tuple-element.12.refs_2_, ...), custom_call_target="tpu_custom_call" | custom-call | tf_op jit(solution)/shard_map/results/pallas_call | solution.py:602

commit v6 on v5

--- a/solution.py
+++ b/solution.py
@@ -508,6 +508,7 @@
     x_last(0)
     for cp in sent[:early]:
         cp.wait_send()
+    later = len(sent)
     y_last(1)
     x_last(1)
     finish_tokens(0, mixed)
@@ -515,9 +516,11 @@
     z_second(1)
     finish_grad(0, gg)
     finish_grad(1, gu)
+    for cp in sent[early:later]:
+        cp.wait_send()
     finish_tokens(1, gtok)
 
-    for cp in sent[early:]:
+    for cp in sent[later:]:
         cp.wait_send()
     for cp in leaving:
         cp.wait()

time: 82.1 us -> 82.1 us (level)
  no operation moved by 1% of the time
where the time goes in v6:
time: 82.1 us; the launch traced here: 82 us
  Pallas kernels  81.4 us (99%)
    pallas_call x1, Pallas kernels, shards(): pl.pallas_call(kernel, out_shape=outs, in_specs=[pl.BlockSpec(memory_spac...  79.5 us
    pallas_call x1, Pallas kernels, shards(): pl.pallas_call(copies, out_shape=outs, in_specs=[pl.BlockSpec(memory_spac...  1.85 us

profile of v6, /device:TPU:1, one launch (start us, length us, event | category | flops | bytes accessed | tf_op | source)
XLA Modules:
  0.0 82.0 jit_solution(6154335980875769022)
XLA Ops:
  0.6 79.5 %layer.1 = (f32[80,256]{1,0:T(8,128)}, f32[80,256]{1,0:T(8,128)}, bf16[256,256]{1,0:T(8,128)(2,1)}, bf16[256,256]{1,0:T(8,128)(2,1)}, bf16[256,256]{1,0:T(8,128)(2,1)}) custom-call(bf16[80,256]{1,0:T(8,128)(2,1)} %tok_hbm.1, bf16[80,256]{1,0:T(8,128)(2,1)} %og_hbm.1, bf16[256,256]{1,0:T(8,128)(2,1)} %gw.1, bf16[256,256]{1,0:T(8,128)(2,1)} %uw.1, ...), custom_call_target="tpu_custom_call" | custom-call | tf_op jit(solution)/shard_map/layer/pallas_call | solution.py:561
  80.2 1.9 %results.1 = (f32[80,256]{1,0:T(8,128)}, f32[80,256]{1,0:T(8,128)}, bf16[256,256]{1,0:T(8,128)(2,1)}, bf16[256,256]{1,0:T(8,128)(2,1)}, bf16[256,256]{1,0:T(8,128)(2,1)}) custom-call(f32[80,256]{1,0:T(8,128)} %get-tuple-element.10.refs_0_, f32[80,256]{1,0:T(8,128)} %get-tuple-element.11.refs_1_, bf16[256,256]{1,0:T(8,128)(2,1)} %get-tuple-element.12.refs_2_, ...), custom_call_target="tpu_custom_call" | custom-call | tf_op jit(solution)/shard_map/results/pallas_call | solution.py:605
